TPU v7x, 256 devices: a whole 4x4x8 slice. The times are simulated.
256 devices in a mesh: dp: 32 (over z, y), mp: 8 (over x, core).
Axes of the slice: x: 4, y: 4, z: 8, core: 2. Of those that a mesh axis runs over, the one named last changes fastest.
Arguments:
- queries: bfloat16 [16384, 2048], P('dp', 'mp'), may hold values from -96 to 96
- out_grad: bfloat16 [16384, 2048], P('dp', 'mp'), may hold values from -0.75 to 0.75
- owner: int32 [256, 2], P('dp'), may hold values from 0 to 31, all different within a row; in each aligned block of 8 rows (0 to 7, 8 to 15, ...) at most 2 rows name the same one
- store_row: int32 [256, 2], P('dp'), may hold values from 0 to 1
- store: bfloat16 [64, 128, 4096], P('dp', None, 'mp'), may hold values from -80 to 80
- norm_gain: bfloat16 [4096], P('mp'), may hold values from 0.5 to 2
- w_key: bfloat16 [4096, 2048], P(None, 'mp'), may hold values from -0.09375 to 0.09375
- w_value: bfloat16 [4096, 2048], P(None, 'mp'), may hold values from -0.09375 to 0.09375
Outputs:
- attended: bfloat16 [16384, 2048], P('dp', 'mp')
- query_grad: bfloat16 [16384, 2048], P('dp', 'mp')
- key_weight_grad: float32 [4096, 2048], P('dp', 'mp')
- value_weight_grad: float32 [4096, 2048], P('dp', 'mp')
Inputs may be any that keep to these rules, and one draw needn't show every extreme that they name: Within the 8 spans of one index of dp no owner is named more than 2 times, and in some such block one owner is named exactly 2 times; the 2 neighbours of a span have different owners.
All inputs are finite; a program needn't handle non-finite values.
Results may differ from a plain program's by a relative error of at most 0.03.
The roundings to bfloat16 on the way count: a program that leaves them out, or rounds other values in their place, can miss the bound.
Values may be sent and summed in bfloat16 or wider, within the bound.
A program may use at most 128 MiB of HBM per device.

v0:
```python
import math

import jax
import jax.numpy as jnp
from jax import lax
from jax.sharding import PartitionSpec as P

HEAD = 128


epsilon = 1e-06


def shards(queries, out_grad, owner, store_row, store, norm_gain, w_key, w_value):
    whole_store, whole_gain = (
        lax.all_gather(store, "mp", axis=2, tiled=True),
        lax.all_gather(norm_gain, "mp", axis=0, tiled=True),
    )
    stored, length, model_width = whole_store.shape
    floats = whole_store.astype(jnp.float32)
    scale_rows = lax.rsqrt(jnp.mean(floats * floats, axis=-1, keepdims=True) + epsilon)
    normed = (
        (floats * scale_rows * whole_gain.astype(jnp.float32))
        .astype(jnp.bfloat16)
        .reshape(stored * length, model_width)
    )
    columns_half = w_key.shape[1]
    key_rows = jnp.dot(normed, w_key, preferred_element_type=jnp.float32).astype(jnp.bfloat16)
    value_rows = jnp.dot(normed, w_value, preferred_element_type=jnp.float32).astype(jnp.bfloat16)
    encoded = jnp.concatenate([key_rows, value_rows], axis=1).reshape(
        stored, length, 2 * columns_half
    )
    spans, neighbours_per = owner.shape
    references = spans * neighbours_per
    peer_count = lax.axis_size("dp")
    own_flat = owner.reshape(references)
    row_flat = store_row.reshape(references)
    global_id = own_flat * stored + row_flat
    earlier = jnp.tril(jnp.ones((references, references), jnp.int32), -1)
    everything = lax.all_gather(encoded, "dp", axis=0, tiled=True)
    context = jnp.take(everything, global_id, axis=0)
    head_size = HEAD
    heads_here = columns_half // head_size
    context_all = context.reshape(spans, neighbours_per * length, 2, heads_here, head_size)
    key_ctx = context_all[:, :, 0]
    value_ctx = context_all[:, :, 1]
    tokens = queries.reshape(spans, -1, heads_here, head_size)
    grads_out = out_grad.reshape(spans, -1, heads_here, head_size)
    inverse_root = 1.0 / math.sqrt(head_size)
    scores = (
        jnp.einsum("cqhd,ckhd->chqk", tokens, key_ctx, preferred_element_type=jnp.float32)
        * inverse_root
    )
    probs = jax.nn.softmax(scores, axis=-1)
    probs_low = probs.astype(jnp.bfloat16)
    attended = (
        jnp.einsum("chqk,ckhd->cqhd", probs_low, value_ctx, preferred_element_type=jnp.float32)
        .astype(jnp.bfloat16)
        .reshape(queries.shape)
    )
    prob_grad = jnp.einsum(
        "cqhd,ckhd->chqk", grads_out, value_ctx, preferred_element_type=jnp.float32
    )
    row_delta = jnp.sum(probs * prob_grad, axis=-1, keepdims=True)
    score_grad = (probs * (prob_grad - row_delta)).astype(jnp.bfloat16)
    query_grad = (
        (
            jnp.einsum("chqk,ckhd->cqhd", score_grad, key_ctx, preferred_element_type=jnp.float32)
            * inverse_root
        )
        .astype(jnp.bfloat16)
        .reshape(queries.shape)
    )
    key_grad = (
        jnp.einsum("chqk,cqhd->ckhd", score_grad, tokens, preferred_element_type=jnp.float32)
        * inverse_root
    )
    value_grad = jnp.einsum(
        "chqk,cqhd->ckhd", probs_low, grads_out, preferred_element_type=jnp.float32
    )
    ref_grads = jnp.stack([key_grad, value_grad], axis=2).reshape(
        references, length, 2 * columns_half
    )
    same_id = (global_id[:, None] == global_id[None, :]).astype(jnp.float32)
    first_use = jnp.sum(same_id * earlier.astype(jnp.float32), axis=1) == 0.0
    summed = jnp.einsum("ij,jtc->itc", same_id, ref_grads, precision=lax.Precision.HIGHEST)
    sent_grads = jnp.where(first_use[:, None, None], summed, 0.0).astype(jnp.bfloat16)
    placement_table = (global_id[:, None] == jnp.arange(peer_count * stored)[None, :]).astype(
        jnp.bfloat16
    )
    dense_grads = jnp.einsum(
        "ir,itc->rtc", placement_table, sent_grads, preferred_element_type=jnp.float32
    )
    row_grad = lax.psum_scatter(
        dense_grads.astype(jnp.bfloat16), "dp", scatter_dimension=0, tiled=True
    )
    row_grad_low = row_grad.reshape(stored * length, 2 * columns_half)
    weight_grad = lax.psum_scatter(
        lax.dot_general(
            normed, row_grad_low, (((0,), (0,)), ((), ())), preferred_element_type=jnp.float32
        ).astype(jnp.bfloat16),
        "dp",
        scatter_dimension=0,
        tiled=True,
    ).astype(jnp.float32)
    return (attended, query_grad, weight_grad[:, :columns_half], weight_grad[:, columns_half:])


def solution(mesh):
    in_specs = (
        P("dp", "mp"),
        P("dp", "mp"),
        P("dp", None),
        P("dp", None),
        P("dp", None, "mp"),
        P("mp"),
        P(None, "mp"),
        P(None, "mp"),
    )
    out_specs = (P("dp", "mp"), P("dp", "mp"), P("dp", "mp"), P("dp", "mp"))
    return jax.shard_map(shards, mesh=mesh, in_specs=in_specs, out_specs=out_specs, check_vma=False)
```

profile of v0, /device:TPU:4, one launch (start us, length us, event | category | flops | bytes accessed | tf_op | source)
XLA Modules:
  0.0 664.1 jit_solution(9272877158265761200)
XLA Ops:
  8.6 12.3 %all-gather = bf16[8,1,512]{2,1,0:T(2,128)(2,1)S(1)} all-gather(bf16[1,1,512]{2,1,0:T(2,128)(2,1)S(1)} %reshape.126), channel_id=1, replica_groups=mesh['dp'=32,'mp'=8] {'mp'}, dimensions={0}, use_global_device_ids=true | all-gather | bytes 9216 | tf_op jit(solution)/shard_map/all_gather | solution.py:17
  21.0 18.5 %all-gather.4.cloned.1.call-done = bf16[2,128,4096]{2,1,0:T(8,128)(2,1)} async-done(((bf16[2,128,512]{2,1,0:T(8,128)(2,1)}), bf16[2,128,4096]{2,1,0:T(8,128)(2,1)}) %all-gather.4.cloned.1.call-update) | async-done | bytes 2097168 | tf_op jit(solution)/shard_map/all_gather | solution.py:16
  39.6 2.2 fusion.1
  48.2 98.6 %all-gather.6.cloned.1.call-done = bf16[64,128,512]{2,1,0:T(8,128)(2,1)} async-done(((bf16[2,128,512]{2,1,0:T(8,128)(2,1)}), bf16[64,128,512]{2,1,0:T(8,128)(2,1)}) %all-gather.6.cloned.1.call-update) | async-done | bytes 8388624 | tf_op jit(solution)/shard_map/all_gather | solution.py:40
  146.7 4.1 gather_fusion
  150.8 2.1 reshape.132
  152.9 2.0 copy_select_fusion
  155.3 1.2 fusion.24
  156.6 4.5 convolution_bitcast_fusion
  161.1 2.0 multiply_reduce_fusion
  165.8 2.3 pad_maximum_fusion
  168.1 5.5 copy.58
  173.6 4.8 reshape.117
  178.4 5.6 copy.59
  184.0 4.4 select_convert_fusion
  188.4 5.6 convolution_convert_fusion
  194.1 11.3 %copy.60 = bf16[64,128,512]{2,1,0:T(8,128)(2,1)} copy(bf16[64,128,512]{2,0,1:T(8,128)(2,1)} %convolution_convert_fusion) | data formatting | bytes 16777216 | tf_op jit(solution)/shard_map/convert_element_type | solution.py:95
  205.7 226.0 %reduce-scatter.3.cloned.1.call-done = bf16[2,128,512]{2,1,0:T(8,128)(2,1)} async-done(((bf16[64,128,512]{2,1,0:T(8,128)(2,1)}), bf16[2,128,512]{2,1,0:T(8,128)(2,1)}) %reduce-scatter.3.cloned.1.call-update) | async-done | bytes 262160 | tf_op jit(solution)/shard_map/reduce_scatter | solution.py:94
  431.7 4.2 bitcast_convert_fusion
  435.9 1.6 copy-done.6
  437.5 1.9 fusion.8
  439.7 1.8 fusion.9
  442.7 213.3 %reduce-scatter.5.cloned.1.call-done = bf16[128,512]{1,0:T(8,128)(2,1)} async-done(((bf16[4096,512]{1,0:T(8,128)(2,1)}), bf16[128,512]{1,0:T(8,128)(2,1)}) %reduce-scatter.5.cloned.1.call-update) | async-done | bytes 131088 | tf_op jit(solution)/shard_map/reduce_scatter | solution.py:98
  656.0 1.6 fusion.23
  (63 shorter events, 12.6 us)
Async XLA Ops:
  7.2 35.3 %copy-start = (bf16[4096,256]{1,0:T(8,128)(2,1)S(1)}, bf16[4096,256]{1,0:T(8,128)(2,1)}, u32[]{:S(2)}) copy-start(bf16[4096,256]{1,0:T(8,128)(2,1)} %param.15) | copy-start | bytes 6291460
  7.2 32.4 %all-gather.4.cloned.1.call-start = ((), (), s32[]{:S(2)}) async-start(), calls=%async_computation.2 | async-start | bytes 2359296 | tf_op jit(solution)/shard_map/all_gather | solution.py:16
  7.9 138.8 %all-gather.6.cloned.1.call-start = ((), (), s32[]{:S(2)}) async-start(), calls=%async_computation.3 | async-start | bytes 8650752 | tf_op jit(solution)/shard_map/all_gather | solution.py:40
  39.6 2.2 copy-start.4
  42.4 1.3 copy-start.2
  42.5 2.3 copy-start.8
  44.8 1.9 copy-start.13
  44.8 1.9 copy-start.14
  44.8 2.2 copy-start.11
  44.8 2.3 copy-start.12
  46.7 385.1 %reduce-scatter.3.cloned.1.call-start = ((), (), s32[]{:S(2)}) async-start(), calls=%async_computation.4 | async-start | bytes 8650752 | tf_op jit(solution)/shard_map/reduce_scatter | solution.py:94
  154.8 6.2 copy-start.5
  161.1 2.0 copy-start.7
  163.4 0.8 copy-start.9
  164.2 1.6 copy-start.10
  205.4 226.3 %copy-start.3 = (bf16[2,128,4096]{2,1,0:T(8,128)(2,1)S(1)}, bf16[2,128,4096]{2,1,0:T(8,128)(2,1)}, u32[]{:S(2)}) copy-start(bf16[2,128,4096]{2,1,0:T(8,128)(2,1)} %copy-done.2) | copy-start | bytes 6291460
  205.4 450.5 %reduce-scatter.5.cloned.1.call-start = ((), (), s32[]{:S(2)}) async-start(), calls=%async_computation.5 | async-start | bytes 4325376 | tf_op jit(solution)/shard_map/reduce_scatter | solution.py:98
  435.9 1.6 copy-start.6
  439.4 218.2 %copy-start.1 = (bf16[4096,256]{1,0:T(8,128)(2,1)S(1)}, bf16[4096,256]{1,0:T(8,128)(2,1)}, u32[]{:S(2)}) copy-start(bf16[4096,256]{1,0:T(8,128)(2,1)} %param.15) | copy-start | bytes 6291460
Sparse Core Ops, SparseCore 0:
  9.9 29.6 all-gather.3
  46.8 99.8 all-gather.5
  205.6 226.1 reduce-scatter.2
  436.1 219.8 reduce-scatter.4
where the time goes:
time: 665 us; the launch traced here: 664 us
  waiting for transfers between devices  557 us (84%)
  local copies, waits for them, and re-layouts  43.8 us (7%)
  matrix products  27.3 us (4%)
  between operations  14 us (2%)
  blocking collectives  12.3 us (2%)
  other arithmetic  8.98 us (1%)
    reduce_scatter x1, waiting for transfers between devices, shards(): lax.psum_scatter(dense_grads.astype(jnp.bfloat16), 'dp', scatter_dimensio...  226 us
    reduce_scatter x1, waiting for transfers between devices, shards(): lax.psum_scatter(lax.dot_general(normed, row_grad_low, (((0,), (0,)), (()...  213 us
    all_gather x1, waiting for transfers between devices, shards(): everything = lax.all_gather(encoded, 'dp', axis=0, tiled=True)  98.6 us
    all_gather x1, waiting for transfers between devices, shards(): lax.all_gather(store, 'mp', axis=2, tiled=True)  18.5 us
  transfers between devices with their start and end apart: 4, of which 4 were waited for; matrix products, arithmetic and copies ran while one was open for 1% of the time, Pallas kernels for 0%

commit v1 on v0

v1 whole, which is shorter than its diff:
```python
import functools
import math

import jax
import jax.numpy as jnp
from jax import lax
from jax.experimental import pallas as pl
from jax.experimental.pallas import tpu as pltpu
from jax.sharding import PartitionSpec as P

MESH = pl.DeviceIdType.MESH
VMEM = pltpu.VMEM
F32, BF16, I32 = jnp.float32, jnp.bfloat16, jnp.int32

HEAD = 128
EPS = 1e-06
NZ, NY, NM = 8, 4, 8
CH = 4
TOK = 32
REFS = 16
GAINROWS = 16
ROWS = 256 + GAINROWS
LIMIT = 56 * 1024 * 1024


def wrap(value, size):
    return lax.rem(value + size, size)


def place():
    d, m = lax.axis_index("dp"), lax.axis_index("mp")
    return lax.div(d, NY), lax.rem(d, NY), m


def remote(src, dst, send, recv, z, y, m):
    return pltpu.make_async_remote_copy(
        src_ref=src, dst_ref=dst, send_sem=send, recv_sem=recv, device_id=(z * NY + y, m), device_id_type=MESH
    )


def greet(peers):
    barrier = pltpu.get_barrier_semaphore()
    for z, y, m in peers:
        pl.semaphore_signal(barrier, inc=1, device_id=(z * NY + y, m), device_id_type=MESH)
    pl.semaphore_wait(barrier, len(peers))


class MpGather:
    def __init__(self, ref, low, high, send, recv):
        self.ref, self.send, self.recv = ref, send, recv
        self.z, self.y, self.m = place()
        self.right, self.left, self.opposite = wrap(self.m + 2, NM), wrap(self.m - 2, NM), wrap(self.m + 4, NM)
        self.twin = self.m + 1 - 2 * lax.rem(self.m, 2)
        self.low, self.high, self.whole = (0, low), (low, high - low), (0, high)

    def copy(self, block, part, target, k):
        piece = self.ref.at[block, pl.ds(*part)]
        return remote(piece, piece, self.send.at[k], self.recv.at[k], self.z, self.y, target)

    def sent(self):
        m, left, right, opposite = self.m, self.left, self.right, self.opposite
        return [
            (m, self.low, right), (m, self.high, right), (m, self.high, left), (m, self.low, left), (m, self.whole, self.twin),
            (left, self.low, right), (right, self.high, left),
            (left, self.whole, self.twin), (right, self.whole, self.twin),
            (opposite, self.low, self.twin), (opposite, self.high, self.twin),
        ]

    def came(self):
        m, left, right, opposite, twin = self.m, self.left, self.right, self.opposite, self.twin
        tl, tr, to = wrap(twin - 2, NM), wrap(twin + 2, NM), wrap(twin + 4, NM)
        return [
            (left, self.low), (left, self.high), (right, self.high), (right, self.low), (twin, self.whole),
            (opposite, self.low), (opposite, self.high),
            (tl, self.whole), (tr, self.whole), (to, self.low), (to, self.high),
        ]

    def start(self, k):
        block, part, target = self.sent()[k]
        self.copy(block, part, target, k).start()

    def arrive(self, k):
        block, part = self.came()[k]
        self.copy(block, part, self.twin, k).wait_recv()

    def finish_send(self, k):
        block, part, target = self.sent()[k]
        self.copy(block, part, target, k).wait_send()

    def step(self, number):
        if number == 0:
            for k in (0, 2, 1, 3, 4):
                self.start(k)
        elif number == 1:
            self.arrive(0)
            self.start(5)
            self.arrive(2)
            self.start(6)
        elif number == 2:
            self.arrive(1)
            self.start(7)
            self.arrive(3)
            self.start(8)
        elif number == 3:
            self.arrive(5)
            self.start(9)
            self.arrive(6)
            self.start(10)
        else:
            for k in (4, 7, 8, 9, 10):
                self.arrive(k)
            for k in range(11):
                self.finish_send(k)

    STEPS = 5


def gather_kernel(store_ref, gain_ref, all_ref, send, recv):
    z, y, m = place()
    moves = MpGather(all_ref, 128, ROWS, send, recv)
    all_ref[m, 0:256] = store_ref[...]
    all_ref[m, 256:ROWS] = jnp.broadcast_to(gain_ref[...], (GAINROWS, 512))
    greet([(z, y, moves.right), (z, y, moves.left), (z, y, moves.twin)])
    for number in range(MpGather.STEPS):
        moves.step(number)


def encode_kernel(all_ref, key_ref, value_ref, kv_ref, turned_ref):
    m = lax.axis_index("mp")
    total = jnp.zeros((256, 1), F32)
    for j in range(NM):
        part = all_ref[j, 0:256].astype(F32)
        total += jnp.sum(part * part, axis=-1, keepdims=True)
    scale = lax.rsqrt(total * (1.0 / 4096.0) + EPS)

    def normed(j):
        gain = all_ref[j, 256:ROWS][0:1].astype(F32)
        return (all_ref[j, 0:256].astype(F32) * scale * gain).astype(BF16)

    keys = jnp.zeros((256, 256), F32)
    values = jnp.zeros((256, 256), F32)
    for j in range(NM):
        block = normed(j)
        keys += jnp.dot(block, key_ref[512 * j : 512 * (j + 1)], preferred_element_type=F32)
        values += jnp.dot(block, value_ref[512 * j : 512 * (j + 1)], preferred_element_type=F32)
    for g in range(4):
        rows = (keys if g < 2 else values)[:, 128 * (g % 2) : 128 * (g % 2) + 128].astype(BF16)
        for n in range(2):
            for t in range(CH):
                first = 128 * n + TOK * t
                kv_ref[g, t, n] = rows[first : first + TOK]
    turned = normed(m).astype(F32).T.astype(BF16)
    for k in range(NY):
        turned_ref[k] = turned[128 * k : 128 * (k + 1)]


def hops(t):
    return (4, 3) if t % 2 == 0 else (3, 4)


def context_kernel(
    kv_ref, turned_ref, owner_ref, row_ref, ctx_ref, normed_ref, table_ref,
    g0, g1, g2, g3, chosen, relay, table_s, near_s, near_r, ring_s, ring_r, out_s, out_r, tab_s, tab_r, turn_s, turn_r, mp_s, mp_r, own_sem,
):
    z, y, m = place()
    chunks = (g0, g1, g2, g3)
    right_y, left_y, far_y = wrap(y + 1, NY), wrap(y - 1, NY), wrap(y + 2, NY)
    up, down = wrap(z + 1, NZ), wrap(z - 1, NZ)
    moves = MpGather(normed_ref, 64, 128, mp_s, mp_r)
    others = (right_y, far_y, left_y)

    ids = owner_ref[...] * 2 + row_ref[...]
    lane = lax.broadcasted_iota(I32, (8, 128), 1)
    span = lax.broadcasted_iota(I32, (8, 128), 0)
    first, second = ids[:, 0:1], ids[:, 1:2]
    match = jnp.minimum(jnp.where(lane == first, 2 * span, REFS), jnp.where(lane == second, 2 * span + 1, REFS))
    table_ref[y, 0:8] = jnp.where(lane == 0, first, second)
    table_ref[y, 8:16] = jnp.broadcast_to(jnp.min(match, axis=0, keepdims=True), (8, 128))

    greet(
        [(z, o, m) for o in others]
        + [(up, y, m), (down, y, m)]
        + [(z, y, moves.right), (z, y, moves.left), (z, y, moves.twin)]
    )

    def near(k, t, source, target):
        return remote(
            kv_ref.at[target, t], chunks[t].at[pl.ds(8 * z + 2 * source, 2)], near_s.at[k, t], near_r.at[k, t], z, target, m
        )

    def tab(k, source, target):
        return remote(table_ref.at[source], table_ref.at[source], tab_s.at[k], tab_r.at[k], z, target, m)

    def turn(k, source, target):
        return remote(
            turned_ref.at[target], normed_ref.at[m, :, pl.ds(pl.multiple_of(256 * source, 256), 256)],
            turn_s.at[k], turn_r.at[k], z, target, m,
        )

    for t in range(CH):
        for k in range(3):
            near(k, t, y, others[k]).start()
    for k in range(3):
        tab(k, y, others[k]).start()
    for k in range(3):
        turn(k, y, others[k]).start()
    for t in range(CH):
        chunks[t][pl.ds(8 * z + 2 * y, 2)] = kv_ref[y, t]
    own_turn = pltpu.make_async_copy(
        turned_ref.at[y], normed_ref.at[m, :, pl.ds(pl.multiple_of(256 * y, 256), 256)], own_sem.at[0]
    )
    own_turn.start()

    def ring(t, direction, h, block, target):
        piece = chunks[t].at[pl.ds(8 * block, 8)]
        return remote(piece, piece, ring_s.at[t, direction, h], ring_r.at[t, direction, h], target, y, m)

    def sender(t, direction, h):
        block = wrap(z - h, NZ) if direction == 0 else wrap(z + h, NZ)
        return ring(t, direction, h, block, up if direction == 0 else down)

    def receiver(t, direction, h):
        block = wrap(z - 1 - h, NZ) if direction == 0 else wrap(z + 1 + h, NZ)
        return ring(t, direction, h, block, up)

    def out(t, k, src, dst, target):
        return remote(src, dst, out_s.at[t, k], out_r.at[t, k], z, target, m)

    def outgoing(t, k):
        if k == 0:
            return out(t, 0, chosen.at[t, 0], ctx_ref.at[y, t], right_y)
        if k == 1:
            return out(t, 1, chosen.at[t, 2], ctx_ref.at[y, t], left_y)
        if k == 2:
            return out(t, 2, chosen.at[t, 1, pl.ds(0, 8)], relay.at[t, 0], right_y)
        if k == 3:
            return out(t, 3, chosen.at[t, 1, pl.ds(8, 8)], relay.at[t, 1], left_y)
        if k == 4:
            return out(t, 4, relay.at[t, 0], ctx_ref.at[left_y, t, pl.ds(0, 8)], right_y)
        return out(t, 5, relay.at[t, 1], ctx_ref.at[right_y, t, pl.ds(8, 8)], left_y)

    def incoming(t, k):
        if k == 0:
            return out(t, 0, chosen.at[t, 0], ctx_ref.at[left_y, t], right_y)
        if k == 1:
            return out(t, 1, chosen.at[t, 2], ctx_ref.at[right_y, t], left_y)
        if k in (2, 3):
            return out(t, k, relay.at[t, k - 2], relay.at[t, k - 2], right_y)
        if k == 4:
            return out(t, 4, relay.at[t, 0], ctx_ref.at[far_y, t, pl.ds(0, 8)], right_y)
        return out(t, 5, relay.at[t, 1], ctx_ref.at[far_y, t, pl.ds(8, 8)], left_y)

    def begin(t):
        for k in range(3):
            near(k, t, wrap(y - 1 - k, NY), y).wait_recv()
        sender(t, 0, 0).start()
        sender(t, 1, 0).start()

    def advance(t, h):
        for direction in (0, 1):
            if h < hops(t)[direction]:
                receiver(t, direction, h).wait_recv()
                if h + 1 < hops(t)[direction]:
                    sender(t, direction, h + 1).start()

    def choose(t):
        if t == 0:
            for k in range(3):
                tab(k, wrap(y - 1 - k, NY), y).wait_recv()
            copy = pltpu.make_async_copy(table_ref, table_s, own_sem.at[1])
            copy.start()
            copy.wait()

        def body(c, carry):
            for n in range(2):
                for k in (2, 1, 3, 0):
                    picked = chunks[t][table_s[wrap(y + k, NY), c, n]]
                    if k == 0:
                        ctx_ref[y, t, 2 * c + n] = picked
                    else:
                        chosen[t, k - 1, 2 * c + n] = picked
            return carry

        lax.fori_loop(0, 8, body, 0)
        for k in (2, 3, 0, 1):
            outgoing(t, k).start()

    def pass_on(t):
        for k in (2, 3):
            incoming(t, k).wait_recv()
            outgoing(t, k + 2).start()

    def begin_mp():
        own_turn.wait()
        for k in range(3):
            turn(k, wrap(y - 1 - k, NY), y).wait_recv()
        moves.step(0)

    events = []
    for t in range(CH):
        events.append((2 * t, 0, functools.partial(begin, t)))
        for h in range(4):
            events.append((2 * t + h + 1, 1, functools.partial(advance, t, h)))
        events.append((2 * t + 4, 2, functools.partial(choose, t)))
        events.append((2 * t + 6, 3, functools.partial(pass_on, t)))
    events.append((1, 4, begin_mp))
    for number in range(1, MpGather.STEPS):
        events.append((2 * number + 4, 4, functools.partial(moves.step, number)))
    for _, _, action in sorted(events, key=lambda event: event[:2]):
        action()
    for t in range(CH):
        for k in (0, 1, 4, 5):
            incoming(t, k).wait_recv()
    for t in range(CH):
        for k in range(6):
            outgoing(t, k).wait_send()
        for k in range(3):
            near(k, t, y, others[k]).wait_send()
        for direction in (0, 1):
            for h in range(hops(t)[direction]):
                sender(t, direction, h).wait_send()
    for k in range(3):
        tab(k, y, others[k]).wait_send()
        turn(k, y, others[k]).wait_send()


def attention_kernel(table_s, q_ref, o_ref, ctx_ref, att_ref, qg_ref, grad_ref, full):
    y = lax.rem(lax.axis_index("dp"), NY)
    root = 1.0 / math.sqrt(HEAD)
    down = (((1,), (1,)), ((), ()))
    across = (((0,), (0,)), ((), ()))
    for c in range(8):
        rows = slice(64 * c, 64 * c + 64)
        for h in range(2):
            columns = slice(128 * h, 128 * h + 128)
            q, o = q_ref[rows, columns], o_ref[rows, columns]
            keys = ctx_ref[h, :, 2 * c : 2 * c + 2].reshape(256, 128)
            values = ctx_ref[2 + h, :, 2 * c : 2 * c + 2].reshape(256, 128)
            scores = lax.dot_general(q, keys, down, preferred_element_type=F32) * root
            weights = jnp.exp(scores - jnp.max(scores, axis=-1, keepdims=True))
            probs = weights / jnp.sum(weights, axis=-1, keepdims=True)
            low = probs.astype(BF16)
            att_ref[rows, columns] = jnp.dot(low, values, preferred_element_type=F32).astype(BF16)
            prob_grad = lax.dot_general(o, values, down, preferred_element_type=F32)
            delta = jnp.sum(probs * prob_grad, axis=-1, keepdims=True)
            score_grad = (probs * (prob_grad - delta)).astype(BF16)
            qg_ref[rows, columns] = (jnp.dot(score_grad, keys, preferred_element_type=F32) * root).astype(BF16)
            key_grad = lax.dot_general(score_grad, q, across, preferred_element_type=F32) * root
            value_grad = lax.dot_general(low, o, across, preferred_element_type=F32)
            for g, grad in ((h, key_grad), (2 + h, value_grad)):
                grad = grad.reshape(CH, 2, TOK, 128)
                full[g, :, 2 * c : 2 * c + 2] = grad
                grad_ref[g, :, 2 * c : 2 * c + 2] = grad.astype(BF16)

    def fold(r, carry):
        first = table_s[y, 8, table_s[y, lax.div(r, 2), lax.rem(r, 2)]]

        @pl.when(first != r)
        def _():
            grad_ref[:, :, first] = (full[:, :, first] + full[:, :, r]).astype(BF16)

        return carry

    lax.fori_loop(0, REFS, fold, 0)


def weight_kernel(
    table_s, grad_ref, normed_ref, key_ref, value_ref,
    r0, r1, r2, r3, relay, dense, ring_up, ring_down, rows, parts, first_up, first_down, sum_up, sum_down,
    out_s, out_r, ring_s, ring_r, near_s, near_r, sum_s, sum_r,
):
    z, y, m = place()
    came = (r0, r1, r2, r3)
    right_y, left_y, far_y = wrap(y + 1, NY), wrap(y - 1, NY), wrap(y + 2, NY)
    up, down = wrap(z + 1, NZ), wrap(z - 1, NZ)
    greet([(z, right_y, m), (z, left_y, m), (up, y, m), (down, y, m)])

    def out(t, k, src, dst, target):
        return remote(src, dst, out_s.at[t, k], out_r.at[t, k], z, target, m)

    def outgoing(t, k):
        if k == 0:
            return out(t, 0, grad_ref.at[right_y, t], came[t].at[y, pl.ds(0, 16)], right_y)
        if k == 1:
            return out(t, 1, grad_ref.at[left_y, t], came[t].at[y, pl.ds(0, 16)], left_y)
        if k == 2:
            return out(t, 2, grad_ref.at[far_y, t, pl.ds(0, 8)], relay.at[t, 0], right_y)
        if k == 3:
            return out(t, 3, grad_ref.at[far_y, t, pl.ds(8, 8)], relay.at[t, 1], left_y)
        if k == 4:
            return out(t, 4, relay.at[t, 0], came[t].at[left_y, pl.ds(0, 8)], right_y)
        return out(t, 5, relay.at[t, 1], came[t].at[right_y, pl.ds(8, 8)], left_y)

    def incoming(t, k):
        if k == 0:
            return out(t, 0, grad_ref.at[y, t], came[t].at[left_y, pl.ds(0, 16)], right_y)
        if k == 1:
            return out(t, 1, grad_ref.at[y, t], came[t].at[right_y, pl.ds(0, 16)], left_y)
        if k in (2, 3):
            return out(t, k, relay.at[t, k - 2], relay.at[t, k - 2], right_y)
        if k == 4:
            return out(t, 4, relay.at[t, 0], came[t].at[far_y, pl.ds(0, 8)], right_y)
        return out(t, 5, relay.at[t, 1], came[t].at[far_y, pl.ds(8, 8)], left_y)

    def post(t):
        for k in (2, 3, 0, 1):
            outgoing(t, k).start()
        came[t][y, pl.ds(0, 16)] = grad_ref[y, t]
        came[t][:, REFS] = jnp.zeros((NY, TOK, 128), BF16)

    def pass_on(t):
        for k in (2, 3):
            incoming(t, k).wait_recv()
            outgoing(t, k + 2).start()

    def block(dest):
        return pl.ds(8 * wrap(dest, NZ), 8)

    def ring(t, direction, h):
        buffers, target = (ring_up, up) if direction == 0 else (ring_down, down)
        count = hops(t)[direction]
        if h == 0:
            src = dense.at[t, block(z + count if direction == 0 else z - count + NZ)]
        else:
            src = buffers.at[t, h - 1]
        return remote(src, buffers.at[t, h], ring_s.at[t, direction, h], ring_r.at[t, direction, h], target, y, m)

    def add_up(t):
        for k in (0, 1, 4, 5):
            incoming(t, k).wait_recv()

        def body(s, carry):
            total = came[t][0, table_s[0, 8, s]].astype(F32)
            for o in range(1, NY):
                total += came[t][o, table_s[o, 8, s]].astype(F32)
            dense[t, s] = total.astype(BF16)
            return carry

        lax.fori_loop(0, 64, body, 0)
        ring(t, 0, 0).start()
        ring(t, 1, 0).start()

    def advance(t, h):
        for direction in (0, 1):
            count = hops(t)[direction]
            if h < count - 1:
                buffers = ring_up if direction == 0 else ring_down
                ring(t, direction, h).wait_recv()
                dest = z + (count - 1 - h) if direction == 0 else z - (count - 1 - h)
                buffers[t, h] = (buffers[t, h].astype(F32) + dense[t, block(dest)].astype(F32)).astype(BF16)
                ring(t, direction, h + 1).start()

    def near(t, k):
        if k == 2:
            source, target = (left_y, right_y) if t % 2 == 0 else (right_y, left_y)
        else:
            source, target = y, (right_y, left_y)[k]
        piece = rows.at[source, :, pl.ds(TOK * t, TOK)]
        return remote(piece, piece, near_s.at[t, k], near_r.at[t, k], z, target, m)

    def near_came(t, k):
        source = (left_y, right_y, far_y)[k]
        piece = rows.at[source, :, pl.ds(TOK * t, TOK)]
        return remote(piece, piece, near_s.at[t, k], near_r.at[t, k], z, right_y, m)

    def settle(t):
        counts = hops(t)
        ring(t, 0, counts[0] - 1).wait_recv()
        ring(t, 1, counts[1] - 1).wait_recv()
        total = (
            dense[t, block(z)].astype(F32)
            + ring_up[t, counts[0] - 1].astype(F32)
            + ring_down[t, counts[1] - 1].astype(F32)
        )
        rows[y, :, pl.ds(TOK * t, TOK)] = total.astype(BF16)
        near(t, 0).start()
        near(t, 1).start()

    def spread(t):
        near_came(t, t % 2).wait_recv()
        near(t, 2).start()

    events = []
    for t in range(CH):
        events.append((2 * t - 1, 0, functools.partial(post, t)))
        events.append((2 * t + 2, 1, functools.partial(pass_on, t)))
        events.append((2 * t + 4, 2, functools.partial(add_up, t)))
        for h in range(3):
            events.append((2 * t + h + 5, 3, functools.partial(advance, t, h)))
        events.append((2 * t + 8, 4, functools.partial(settle, t)))
        events.append((2 * t + 9, 5, functools.partial(spread, t)))
    for _, _, action in sorted(events, key=lambda event: event[:2]):
        action()
    for t in range(CH):
        near_came(t, 1 - t % 2).wait_recv()
        near_came(t, 2).wait_recv()

    row_grad = jnp.concatenate([rows[g].reshape(1024, 128) for g in range(4)], axis=1)

    def partial_of(dest):
        parts[wrap(dest, NZ)] = jnp.dot(normed_ref[wrap(dest, NZ)], row_grad, preferred_element_type=F32)

    def half(index):
        return slice(256 * index, 256 * index + 256)

    def sums(part, direction, h):
        buffers, firsts, target = (sum_up, first_up, up) if direction == 0 else (sum_down, first_down, down)
        src = firsts.at[part] if h == 0 else buffers.at[part, h - 1]
        return remote(src, buffers.at[part, h], sum_s.at[part, direction, h], sum_r.at[part, direction, h], target, y, m)

    def set_out(part, direction):
        count = hops(part)[direction]
        dest = z + count if direction == 0 else z - count
        (first_up if direction == 0 else first_down)[part] = parts[wrap(dest, NZ), :, half(part)].astype(BF16)
        sums(part, direction, 0).start()

    def hand_on(part, direction, h):
        count = hops(part)[direction]
        if h < count - 1:
            buffers = sum_up if direction == 0 else sum_down
            sums(part, direction, h).wait_recv()
            dest = z + (count - 1 - h) if direction == 0 else z - (count - 1 - h)
            buffers[part, h] = (buffers[part, h].astype(F32) + parts[wrap(dest, NZ), :, half(part)]).astype(BF16)
            sums(part, direction, h + 1).start()

    partial_of(z + 4)
    set_out(0, 0)
    set_out(1, 1)
    partial_of(z + 3)
    set_out(1, 0)
    partial_of(z - 3)
    set_out(0, 1)
    for h in range(3):
        if h < 2:
            partial_of(z + 2 - h)
            partial_of(z - 2 + h)
        else:
            partial_of(z)
        for part, direction in ((0, 0), (1, 1), (1, 0), (0, 1)):
            hand_on(part, direction, h)
    for part, ref in ((0, key_ref), (1, value_ref)):
        counts = hops(part)
        sums(part, 0, counts[0] - 1).wait_recv()
        sums(part, 1, counts[1] - 1).wait_recv()
        ref[...] = (
            parts[z, :, half(part)]
            + sum_up[part, counts[0] - 1].astype(F32)
            + sum_down[part, counts[1] - 1].astype(F32)
        )

    for t in range(CH):
        for k in range(6):
            outgoing(t, k).wait_send()
        for k in range(3):
            near(t, k).wait_send()
        for direction in (0, 1):
            for h in range(hops(t)[direction]):
                ring(t, direction, h).wait_send()
    for part in (0, 1):
        for direction in (0, 1):
            for h in range(hops(part)[direction]):
                sums(part, direction, h).wait_send()


def in_vmem(count):
    return [pl.BlockSpec(memory_space=VMEM)] * count


IN_SMEM = pl.BlockSpec(memory_space=pltpu.SMEM)


def dma(*shape):
    return pltpu.SemaphoreType.DMA(shape)


def talk(number):
    return pltpu.CompilerParams(collective_id=number, has_side_effects=True, vmem_limit_bytes=LIMIT)


def gather_features(store, gain):
    return pl.pallas_call(
        gather_kernel,
        out_shape=jax.ShapeDtypeStruct((NM, ROWS, 512), BF16),
        in_specs=in_vmem(2),
        out_specs=in_vmem(1)[0],
        scratch_shapes=[dma(11), dma(11)],
        compiler_params=talk(0),
        name="gather_features",
    )(store, gain)


def encode(everything, w_key, w_value):
    return pl.pallas_call(
        encode_kernel,
        out_shape=(jax.ShapeDtypeStruct((4, CH, 2, TOK, 128), BF16), jax.ShapeDtypeStruct((NY, 128, 256), BF16)),
        in_specs=in_vmem(3),
        out_specs=tuple(in_vmem(2)),
        compiler_params=pltpu.CompilerParams(vmem_limit_bytes=LIMIT),
        name="encode",
    )(everything, w_key, w_value)


def fetch_context(kv, turned, owner, store_row):
    return pl.pallas_call(
        context_kernel,
        out_shape=(
            jax.ShapeDtypeStruct((4, CH, REFS, TOK, 128), BF16),
            jax.ShapeDtypeStruct((NM, 128, 1024), BF16),
            jax.ShapeDtypeStruct((NY, 16, 128), I32),
        ),
        in_specs=in_vmem(4),
        out_specs=tuple(in_vmem(3)),
        scratch_shapes=[VMEM((64, TOK, 128), BF16)] * CH
        + [
            VMEM((CH, 3, REFS, TOK, 128), BF16),
            VMEM((CH, 2, 8, TOK, 128), BF16),
            pltpu.SMEM((NY, 16, 128), I32),
            dma(3, CH), dma(3, CH), dma(CH, 2, 4), dma(CH, 2, 4), dma(CH, 6), dma(CH, 6),
            dma(3), dma(3), dma(3), dma(3), dma(11), dma(11), dma(2),
        ],
        compiler_params=talk(1),
        name="fetch_context",
    )(kv, turned, owner, store_row)


def attention(table, queries, out_grad, context):
    return pl.pallas_call(
        attention_kernel,
        out_shape=(
            jax.ShapeDtypeStruct(queries.shape, BF16),
            jax.ShapeDtypeStruct(queries.shape, BF16),
            jax.ShapeDtypeStruct((4, CH, REFS, TOK, 128), BF16),
        ),
        in_specs=[IN_SMEM] + in_vmem(3),
        out_specs=tuple(in_vmem(3)),
        scratch_shapes=[VMEM((4, CH, REFS, TOK, 128), F32)],
        compiler_params=pltpu.CompilerParams(vmem_limit_bytes=LIMIT),
        name="attention",
    )(table, queries, out_grad, context)


def weight_grads(table, grads, normed):
    return pl.pallas_call(
        weight_kernel,
        out_shape=(jax.ShapeDtypeStruct((128, 256), F32), jax.ShapeDtypeStruct((128, 256), F32)),
        in_specs=[IN_SMEM] + in_vmem(2),
        out_specs=tuple(in_vmem(2)),
        scratch_shapes=[VMEM((NY, REFS + 1, TOK, 128), BF16)] * CH
        + [
            VMEM((CH, 2, 8, TOK, 128), BF16),
            VMEM((CH, 64, TOK, 128), BF16),
            VMEM((CH, 4, 8, TOK, 128), BF16),
            VMEM((CH, 4, 8, TOK, 128), BF16),
            VMEM((4, 8, 128, 128), BF16),
            VMEM((NZ, 128, 512), F32),
            VMEM((2, 128, 256), BF16),
            VMEM((2, 128, 256), BF16),
            VMEM((2, 4, 128, 256), BF16),
            VMEM((2, 4, 128, 256), BF16),
            dma(CH, 6), dma(CH, 6), dma(CH, 2, 4), dma(CH, 2, 4), dma(CH, 3), dma(CH, 3), dma(2, 2, 4), dma(2, 2, 4),
        ],
        compiler_params=talk(2),
        name="weight_grads",
    )(table, grads, normed)


def shards(queries, out_grad, owner, store_row, store, norm_gain, w_key, w_value):
    everything = gather_features(store.reshape(256, 512), norm_gain.reshape(1, 512))
    kv, turned = encode(everything, w_key, w_value)
    context, normed, table = fetch_context(kv, turned, owner, store_row)
    attended, query_grad, grads = attention(table, queries, out_grad, context)
    key_weight_grad, value_weight_grad = weight_grads(table, grads, normed)
    return (attended, query_grad, key_weight_grad, value_weight_grad)


def solution(mesh):
    in_specs = (
        P("dp", "mp"),
        P("dp", "mp"),
        P("dp", None),
        P("dp", None),
        P("dp", None, "mp"),
        P("mp"),
        P(None, "mp"),
        P(None, "mp"),
    )
    out_specs = (P("dp", "mp"), P("dp", "mp"), P("dp", "mp"), P("dp", "mp"))
    return jax.shard_map(shards, mesh=mesh, in_specs=in_specs, out_specs=out_specs, check_vma=False)
```

time: 665 us -> 185 us (0.28)
  waiting for transfers between devices: 557 us -> 0 us
  Pallas kernels: 0 us -> 174 us
  local copies, waits for them, and re-layouts: 43.8 us -> 7.08 us
  matrix products: 27.3 us -> 0 us
  between operations: 14 us -> 0.66 us
  blocking collectives: 12.3 us -> 0 us
  other arithmetic: 8.98 us -> 0 us
    reduce_scatter x2 -> x0, waiting for transfers between devices: 439 us -> none  [the longest x1 226 us: shards(): lax.psum_scatter(dense_grads.astype(jnp.bfloat16), 'dp', scatter_dimensio...]
    pallas_call x0 -> x5, Pallas kernels: none -> 174 us  [the longest x1 79.6 us: weight_grads(): pl.pallas_call(weight_kernel, out_shape=(jax.ShapeDtypeStruct((128, 256),...]
    all_gather x2 -> x0, waiting for transfers between devices: 117 us -> none  [the longest x1 98.6 us: shards(): everything = lax.all_gather(encoded, 'dp', axis=0, tiled=True)]
    dot_general x11 -> x0, matrix products: 27.3 us -> none  [the longest x1 5.65 us: shards(): jnp.einsum('ir,itc->rtc', placement_table, sent_grads, preferred_element_...]
    all_gather x1 -> x0, blocking collectives: 12.3 us -> none  [shards(): lax.all_gather(norm_gain, 'mp', axis=0, tiled=True)]
    convert_element_type x3 -> x0, local copies, waits for them, and re-layouts: 11.9 us -> none  [the longest x1 11.3 us: shards(): dense_grads.astype(jnp.bfloat16)]
    reshape x6 -> x1, local copies, waits for them, and re-layouts: 12.9 us -> 1.26 us  [shards(): norm_gain.reshape(1, 512)]
  transfers between devices with their start and end apart: 4 -> 0, of which waited for: 4 -> 0; matrix products, arithmetic and copies ran while one was open for 1% -> 0% of each run, Pallas kernels for 0% -> 0%
where the time goes in v1:
time: 185 us; the launch traced here: 181 us
  Pallas kernels  174 us (94%)
  local copies, waits for them, and re-layouts  7.08 us (4%)
    pallas_call x1, Pallas kernels, weight_grads(): pl.pallas_call(weight_kernel, out_shape=(jax.ShapeDtypeStruct((128, 256),...  79.6 us
    pallas_call x1, Pallas kernels, fetch_context(): pl.pallas_call(context_kernel, out_shape=(jax.ShapeDtypeStruct((4, CH, RE...  61.5 us
    pallas_call x1, Pallas kernels, gather_features(): pl.pallas_call(gather_kernel, out_shape=jax.ShapeDtypeStruct((NM, ROWS, 5...  15.8 us
    pallas_call x1, Pallas kernels, attention(): pl.pallas_call(attention_kernel, out_shape=(jax.ShapeDtypeStruct(queries....  11.5 us
    unnamed x4, local copies, waits for them, and re-layouts  5.82 us
    pallas_call x1, Pallas kernels, encode(): pl.pallas_call(encode_kernel, out_shape=(jax.ShapeDtypeStruct((4, CH, 2,...  5.28 us

profile of v1, /device:TPU:4, one launch (start us, length us, event | category | flops | bytes accessed | tf_op | source)
XLA Modules:
  0.0 181.4 jit_solution(12344464252080835465)
XLA Ops:
  0.6 1.3 reshape.15.gain_ref
  1.9 1.3 copy.12.owner_ref
  3.2 1.3 copy.13.row_ref
  4.6 15.8 %gather_features.1.all_ref = bf16[8,272,512]{2,1,0:T(8,128)(2,1)} custom-call(bf16[256,512]{1,0:T(8,128)(2,1)} %bitcast.1, bf16[1,512]{1,0:T(2,128)(2,1)} %reshape.15.gain_ref), custom_call_target="tpu_custom_call" | custom-call | tf_op jit(solution)/shard_map/gather_features/pallas_call | solution.py:581
  20.4 5.3 %encode.1 = (bf16[4,4,2,32,128]{4,3,2,1,0:T(8,128)(2,1)}, bf16[4,128,256]{2,1,0:T(8,128)(2,1)}) custom-call(bf16[8,272,512]{2,1,0:T(8,128)(2,1)} %gather_features.1.all_ref, bf16[4096,256]{1,0:T(8,128)(2,1)} %key_ref.1, bf16[4096,256]{1,0:T(8,128)(2,1)} %value_ref.1), custom_call_target="tpu_custom_call" | custom-call | tf_op jit(solution)/shard_map/encode/pallas_call | solution.py:593
  25.7 61.5 %fetch_context.1 = (bf16[4,4,16,32,128]{4,3,2,1,0:T(8,128)(2,1)}, bf16[8,128,1024]{2,1,0:T(8,128)(2,1)}, s32[4,16,128]{2,1,0:T(8,128)}) custom-call(bf16[4,4,2,32,128]{4,3,2,1,0:T(8,128)(2,1)} %get-tuple-element.14.kv_ref, bf16[4,128,256]{2,1,0:T(8,128)(2,1)} %get-tuple-element.15.turned_ref, s32[8,2]{1,0:T(8,128)} %copy.12.owner_ref, s32[8,2]{1,0:T(8,128)} %copy.13.row_ref), custom_call_target="tpu_custom_call" | custom-call | tf_op jit(solution)/shard_map/fetch_context/pallas_call | solution.py:604
  87.2 11.5 %attention.1 = (bf16[512,256]{1,0:T(8,128)(2,1)}, bf16[512,256]{1,0:T(8,128)(2,1)}, bf16[4,4,16,32,128]{4,3,2,1,0:T(8,128)(2,1)}) custom-call(s32[4,16,128]{2,1,0:T(8,128)} %get-tuple-element.16.table_s, bf16[512,256]{1,0:T(8,128)(2,1)} %q_ref.1, bf16[512,256]{1,0:T(8,128)(2,1)} %o_ref.1, bf16[4,4,16,32,128]{4,3,2,1,0:T(8,128)(2,1)} %get-tuple-element.17.ctx_ref), custom_call_target="tpu_custom_call" | custom-call | tf_op jit(solution)/shard_map/attention/pallas_call | solution.py:627
  98.6 79.6 %weight_grads.1 = (f32[128,256]{1,0:T(8,128)}, f32[128,256]{1,0:T(8,128)}) custom-call(s32[4,16,128]{2,1,0:T(8,128)} %get-tuple-element.16.table_s, bf16[4,4,16,32,128]{4,3,2,1,0:T(8,128)(2,1)} %get-tuple-element.20.grad_ref, bf16[8,128,1024]{2,1,0:T(8,128)(2,1)} %get-tuple-element.21.normed_ref), custom_call_target="tpu_custom_call" | custom-call | tf_op jit(solution)/shard_map/weight_grads/pallas_call | solution.py:643
  178.2 1.6 copy.16
  179.8 1.6 copy.17

commit v2 on v0

v2 whole, which is shorter than its diff:
```python
import math

import jax
import jax.numpy as jnp
from jax import lax
from jax.experimental import pallas as pl
from jax.experimental.pallas import tpu as pltpu
from jax.sharding import PartitionSpec as P

MESH = pl.DeviceIdType.MESH
VMEM, SMEM = pltpu.VMEM, pltpu.SMEM
F32, BF16, I32 = jnp.float32, jnp.bfloat16, jnp.int32

HEAD = 128
ROOT = 1.0 / math.sqrt(HEAD)
EPS = 1e-06
NZ, NY, NM = 8, 4, 8
TOK = 32
REFS = 16
NONE = REFS
FLOOR = -3.0e38
DOWN = (((1,), (1,)), ((), ()))
ACROSS = (((0,), (0,)), ((), ()))
ORDER = (2, 1, 3)


def wrap(value, size):
    return lax.rem(value + size, size)


def place():
    d, m = lax.axis_index("dp"), lax.axis_index("mp")
    return lax.div(d, NY), lax.rem(d, NY), m


def remote(src, dst, send, recv, target):
    z, y, m = target
    return pltpu.make_async_remote_copy(
        src_ref=src, dst_ref=dst, send_sem=send, recv_sem=recv, device_id=(z * NY + y, m), device_id_type=MESH
    )


def greet(peers):
    barrier = pltpu.get_barrier_semaphore()
    for z, y, m in peers:
        pl.semaphore_signal(barrier, inc=1, device_id=(z * NY + y, m), device_id_type=MESH)
    return lambda: pl.semaphore_wait(barrier, len(peers))


class MpGather:
    def __init__(self, ref, low, high, send, recv):
        self.ref, self.send, self.recv = ref, send, recv
        self.z, self.y, self.m = place()
        self.right, self.left, self.opposite = wrap(self.m + 2, NM), wrap(self.m - 2, NM), wrap(self.m + 4, NM)
        self.twin = self.m + 1 - 2 * lax.rem(self.m, 2)
        self.low, self.high, self.whole = (0, low), (low, high - low), (0, high)

    def copy(self, block, part, target, k):
        piece = self.ref.at[block, pl.ds(*part)]
        return remote(piece, piece, self.send.at[k], self.recv.at[k], (self.z, self.y, target))

    def sent(self):
        m, left, right, opposite = self.m, self.left, self.right, self.opposite
        return [
            (m, self.low, right), (m, self.high, right), (m, self.high, left), (m, self.low, left), (m, self.whole, self.twin),
            (left, self.low, right), (right, self.high, left),
            (left, self.whole, self.twin), (right, self.whole, self.twin),
            (opposite, self.low, self.twin), (opposite, self.high, self.twin),
        ]

    def came(self):
        left, right, opposite, twin = self.left, self.right, self.opposite, self.twin
        tl, tr, to = wrap(twin - 2, NM), wrap(twin + 2, NM), wrap(twin + 4, NM)
        return [
            (left, self.low), (left, self.high), (right, self.high), (right, self.low), (twin, self.whole),
            (opposite, self.low), (opposite, self.high),
            (tl, self.whole), (tr, self.whole), (to, self.low), (to, self.high),
        ]

    def start(self, k):
        block, part, target = self.sent()[k]
        self.copy(block, part, target, k).start()

    def arrive(self, k):
        block, part = self.came()[k]
        self.copy(block, part, self.twin, k).wait_recv()

    def finish_send(self, k):
        block, part, target = self.sent()[k]
        self.copy(block, part, target, k).wait_send()

    def step(self, number):
        if number == 0:
            for k in (0, 2, 1, 3, 4):
                self.start(k)
        elif number == 1:
            self.arrive(0)
            self.start(5)
            self.arrive(2)
            self.start(6)
        elif number == 2:
            self.arrive(1)
            self.start(7)
            self.arrive(3)
            self.start(8)
        elif number == 3:
            self.arrive(5)
            self.start(9)
            self.arrive(6)
            self.start(10)
        else:
            for k in (4, 7, 8, 9, 10):
                self.arrive(k)
            for k in range(11):
                self.finish_send(k)


def counts(g):
    return (4, 3) if g % 2 == 0 else (3, 4)


def kernel(
    owner_s, row_s, q_hbm, o_hbm, store_hbm, gain_ref, key_hbm, value_hbm,
    att_ref, qg_ref, kw_ref, vw_ref,
    every, gains, w_key, w_value, table, table_s, qo, turned, normed, g0, g1, g2, g3,
    e_buf, pg_buf, stats, own_part, sent_part, came_part, f0, f1, f2, f3,
    dense, ring_up, ring_down, rows, parts, first_up, first_down, sum_up, sum_down,
    local, store_sems, gain_sems, tab_sems, qo_sems, every_s, every_r, turn_sems, normed_s, normed_r,
    ring_sems, stat_sems, back_sems, part_sems, row_sems, sum_sems,
):
    z, y, m = place()
    chunks, full = (g0, g1, g2, g3), (f0, f1, f2, f3)
    up, down = (wrap(z + 1, NZ), y, m), (wrap(z - 1, NZ), y, m)
    first_moves = MpGather(every, 4, 8, every_s, every_r)
    second_moves = MpGather(normed, 64, 128, normed_s, normed_r)

    def at_y(k):
        return wrap(y + k, NY)

    def from_y(k):
        return wrap(y - k, NY)

    def peer(k):
        return (z, at_y(k), m)

    met = greet(
        [peer(k) for k in (1, 2, 3)] + [up, down] + [(z, y, wrap(m + k, NM)) for k in range(1, NM)]
    )

    def at_home():
        quarter = pl.ds(pl.multiple_of(TOK * y, TOK), TOK)
        copies = [
            pltpu.make_async_copy(store_hbm.at[:, quarter], every.at[m, pl.ds(2 * y, 2)], local.at[0]),
            pltpu.make_async_copy(key_hbm, w_key, local.at[1]),
            pltpu.make_async_copy(value_hbm, w_value, local.at[2]),
        ]
        for h in range(2):
            for i, ref in enumerate((q_hbm, o_hbm)):
                copies.append(
                    pltpu.make_async_copy(ref.at[:, pl.ds(HEAD * h, HEAD)], qo.at[h, y, i], local.at[3 + 2 * h + i])
                )
        return copies

    home = at_home()
    for copy in home:
        copy.start()

    lane = lax.broadcasted_iota(I32, (8, 128), 1)
    line = lax.broadcasted_iota(I32, (8, 128), 0)
    ids = jnp.zeros((8, 128), I32)
    first = jnp.full((8, 128), NONE, I32)
    last = jnp.full((8, 128), -1, I32)
    for r in range(REFS):
        name = owner_s[r % 2, r // 2] * 2 + row_s[r % 2, r // 2]
        ids = jnp.where(lane == r, name, ids)
        first = jnp.where(lane == name, jnp.minimum(first, r), first)
        last = jnp.where(lane == name, r, last)
    second = jnp.where(last > first, last, NONE)
    table[y] = jnp.where(line == 0, ids, jnp.where(line == 1, first, second))
    gains[m] = jnp.broadcast_to(gain_ref[...].reshape(1, 512), (16, 512))
    for g in range(4):
        full[g][:, NONE] = jnp.zeros((NY, TOK, HEAD), F32)
    stats[:, y] = jnp.zeros((2, NY, 16, 128), F32)

    def store_copy(k, source, target):
        quarter = pl.ds(pl.multiple_of(TOK * target[1], TOK), TOK)
        return remote(
            store_hbm.at[:, quarter], every.at[m, pl.ds(2 * source, 2)], store_sems.at[0, k - 1], store_sems.at[1, k - 1], target
        )

    def gain_copy(k, source, target):
        return remote(gains.at[source], gains.at[source], gain_sems.at[0, k - 1], gain_sems.at[1, k - 1], (z, y, target))

    def tab_copy(k, source):
        return remote(table.at[source], table.at[source], tab_sems.at[0, k - 1], tab_sems.at[1, k - 1], peer(k))

    def qo_copy(h, i, k, source):
        ref = (q_hbm, o_hbm)[i]
        return remote(
            ref.at[:, pl.ds(HEAD * h, HEAD)], qo.at[h, source, i], qo_sems.at[0, h, i, k - 1], qo_sems.at[1, h, i, k - 1], peer(k)
        )

    met()
    for k in ORDER:
        store_copy(k, y, peer(k)).start()
    for k in range(1, NM):
        gain_copy(k, m, wrap(m + k, NM)).start()
    for k in ORDER:
        tab_copy(k, y).start()
    home[0].wait()
    for k in ORDER:
        store_copy(k, from_y(k), (z, y, m)).wait_recv()
    first_moves.step(0)
    for h in range(2):
        for k in ORDER:
            for i in range(2):
                qo_copy(h, i, k, y).start()
    for k in ORDER:
        tab_copy(k, from_y(k)).wait_recv()
    to_scalars = pltpu.make_async_copy(table, table_s, local.at[7])
    to_scalars.start()
    first_moves.step(1)
    first_moves.step(2)
    first_moves.step(3)
    first_moves.step(4)
    for k in range(1, NM):
        gain_copy(k, wrap(m - k, NM), m).wait_recv()
    home[1].wait()
    home[2].wait()

    total = jnp.zeros((256, 1), F32)
    for j in range(NM):
        part = every[j].reshape(256, 512).astype(F32)
        total += jnp.sum(part * part, axis=-1, keepdims=True)
    scale = lax.rsqrt(total * (1.0 / 4096.0) + EPS)
    for j in range(NM):
        gain = gains[j][0:1].astype(F32)
        block = every[j].reshape(256, 512).astype(F32) * scale * gain
        every[j] = block.astype(BF16).reshape(8, TOK, 512)

    def encode(h):
        encoded = jnp.zeros((256, 256), F32)
        for j in range(NM):
            depth, columns = slice(512 * j, 512 * (j + 1)), slice(HEAD * h, HEAD * (h + 1))
            weights = jnp.concatenate([w_key[depth, columns], w_value[depth, columns]], axis=1)
            encoded += jnp.dot(every[j].reshape(256, 512), weights, preferred_element_type=F32)
        for i in range(2):
            chunks[2 * h + i][pl.ds(8 * z, 8)] = encoded[:, HEAD * i : HEAD * (i + 1)].astype(BF16).reshape(8, TOK, HEAD)

    def ring_copy(g, direction, h, block):
        piece = chunks[g].at[pl.ds(8 * block, 8)]
        return remote(
            piece, piece, ring_sems.at[0, g, direction, h], ring_sems.at[1, g, direction, h], (up, down)[direction]
        )

    def ring_sent(g, direction, h):
        return ring_copy(g, direction, h, wrap(z - h, NZ) if direction == 0 else wrap(z + h, NZ))

    def ring_came(g, direction, h):
        return ring_copy(g, direction, h, wrap(z - 1 - h, NZ) if direction == 0 else wrap(z + 1 + h, NZ))

    def launch(g):
        for direction in (0, 1):
            ring_sent(g, direction, 0).start()

    def advance(g, h):
        for direction in (0, 1):
            if h < counts(g)[direction]:
                ring_came(g, direction, h).wait_recv()
                if h + 1 < counts(g)[direction]:
                    ring_sent(g, direction, h + 1).start()

    def turn_copy(k, source):
        lanes = pl.ds(pl.multiple_of(256 * source, 256), 256)
        return remote(
            turned.at[at_y(k)], normed.at[m, :, lanes], turn_sems.at[0, k - 1], turn_sems.at[1, k - 1], peer(k)
        )

    def turn():
        flat = every[m].reshape(256, 512).astype(F32).T.astype(BF16)
        for i in range(NY):
            turned[i] = flat[128 * i : 128 * (i + 1)]
        for k in ORDER:
            turn_copy(k, y).start()
        copy = pltpu.make_async_copy(turned.at[y], normed.at[m, :, pl.ds(pl.multiple_of(256 * y, 256), 256)], local.at[8])
        copy.start()
        copy.wait()

    context_span = lax.div(lax.broadcasted_iota(I32, (128, 128), 0), 64)
    query_span = lax.div(lax.broadcasted_iota(I32, (128, 128), 1), 64)
    same = context_span == query_span

    def context(g, b, p):
        picked = [chunks[g][table_s[b, 0, 4 * p + i]] for i in range(4)]
        return jnp.concatenate(picked, axis=0)

    def score(h, k):
        b = at_y(k)
        for p in range(4):
            queries, grads = qo[h, b, 0, 128 * p : 128 * (p + 1)], qo[h, b, 1, 128 * p : 128 * (p + 1)]
            scores = lax.dot_general(context(2 * h, b, p), queries, DOWN, preferred_element_type=F32) * ROOT
            scores = jnp.where(same, scores, FLOOR)
            prob_grad = lax.dot_general(context(2 * h + 1, b, p), grads, DOWN, preferred_element_type=F32)
            top = jnp.max(scores, axis=0, keepdims=True)
            weights = jnp.exp(scores - top)
            e_buf[h, k, p] = weights
            pg_buf[h, k, p] = prob_grad
            stats[h, y, b, p : p + 1] = top
            stats[h, y, b, 4 + p : 5 + p] = jnp.sum(weights, axis=0, keepdims=True)
            stats[h, y, b, 8 + p : 9 + p] = jnp.sum(weights * prob_grad, axis=0, keepdims=True)

    def stat_copy(h, k, source):
        piece = stats.at[h, source]
        return remote(piece, piece, stat_sems.at[0, h, k - 1], stat_sems.at[1, h, k - 1], peer(k))

    def part_copy(h, k):
        return remote(
            sent_part.at[h, k - 1], came_part.at[h, k - 1], part_sems.at[0, h, k - 1], part_sems.at[1, h, k - 1], peer(k)
        )

    def grads_of(h, k):
        b = at_y(k)
        tops = [stats[h, s, b, 0:4] for s in range(NY)]
        top = jnp.maximum(jnp.maximum(tops[0], tops[1]), jnp.maximum(tops[2], tops[3]))
        shares = [jnp.exp(each - top) for each in tops]
        whole, moment = jnp.zeros((4, 128), F32), jnp.zeros((4, 128), F32)
        for s in range(NY):
            whole += shares[s] * stats[h, s, b, 4:8]
            moment += shares[s] * stats[h, s, b, 8:12]
        factor = jnp.exp(stats[h, y, b, 0:4] - top) / whole
        delta = moment / whole
        for p in range(4):
            lines = slice(128 * p, 128 * (p + 1))
            queries, grads = qo[h, b, 0, lines], qo[h, b, 1, lines]
            keys, values = context(2 * h, b, p), context(2 * h + 1, b, p)
            probs = e_buf[h, k, p] * factor[p : p + 1]
            low = probs.astype(BF16)
            score_grad = (probs * (pg_buf[h, k, p] - delta[p : p + 1])).astype(BF16)
            attended = lax.dot_general(low, values, ACROSS, preferred_element_type=F32)
            query_grad = lax.dot_general(score_grad, keys, ACROSS, preferred_element_type=F32) * ROOT
            if k == 0:
                own_part[h, 0, lines] = attended
                own_part[h, 1, lines] = query_grad
            else:
                sent_part[h, k - 1, 0, lines] = attended.astype(BF16)
                sent_part[h, k - 1, 1, lines] = query_grad.astype(BF16)
            key_grad = jnp.dot(score_grad, queries, preferred_element_type=F32) * ROOT
            value_grad = jnp.dot(low, grads, preferred_element_type=F32)
            full[2 * h][b, 4 * p : 4 * p + 4] = key_grad.reshape(4, TOK, HEAD)
            full[2 * h + 1][b, 4 * p : 4 * p + 4] = value_grad.reshape(4, TOK, HEAD)
        if k > 0:
            part_copy(h, k).start()

    def outputs(h):
        for k in ORDER:
            part_copy(h, k).wait_recv()
        for i, ref in ((0, att_ref), (1, qg_ref)):
            whole = own_part[h, i]
            for k in ORDER:
                whole += came_part[h, k - 1, i].astype(F32)
            ref[:, HEAD * h : HEAD * (h + 1)] = whole.astype(BF16)

    def block(dest):
        return pl.ds(8 * wrap(dest, NZ), 8)

    def back_copy(g, direction, h):
        buffers, target = ((ring_up, up), (ring_down, down))[direction]
        count = counts(g)[direction]
        if h == 0:
            src = dense.at[g, block(z + count if direction == 0 else z - count)]
        else:
            src = buffers.at[g, h - 1]
        return remote(src, buffers.at[g, h], back_sems.at[0, g, direction, h], back_sems.at[1, g, direction, h], target)

    def add_up(g):
        def body(s, carry):
            whole = full[g][0, table_s[0, 1, s]] + full[g][0, table_s[0, 2, s]]
            for b in range(1, NY):
                whole += full[g][b, table_s[b, 1, s]] + full[g][b, table_s[b, 2, s]]
            dense[g, s] = whole.astype(BF16)
            return carry

        lax.fori_loop(0, 64, body, 0, unroll=4)
        for direction in (0, 1):
            back_copy(g, direction, 0).start()

    def pass_back(g, h):
        for direction in (0, 1):
            count = counts(g)[direction]
            if h < count - 1:
                buffers = (ring_up, ring_down)[direction]
                back_copy(g, direction, h).wait_recv()
                dest = z + (count - 1 - h) if direction == 0 else z - (count - 1 - h)
                buffers[g, h] = (buffers[g, h].astype(F32) + dense[g, block(dest)].astype(F32)).astype(BF16)
                back_copy(g, direction, h + 1).start()

    def row_copy(g, k, source):
        piece = rows.at[source, g]
        return remote(piece, piece, row_sems.at[0, g, k - 1], row_sems.at[1, g, k - 1], peer(k))

    def settle(g):
        n_up, n_down = counts(g)
        back_copy(g, 0, n_up - 1).wait_recv()
        back_copy(g, 1, n_down - 1).wait_recv()
        whole = dense[g, block(z)].astype(F32) + ring_up[g, n_up - 1].astype(F32) + ring_down[g, n_down - 1].astype(F32)
        rows[y, g] = whole.astype(BF16).reshape(256, HEAD)
        for k in ORDER:
            row_copy(g, k, y).start()

    def sum_copy(h, direction, n):
        buffers, firsts, target = ((sum_up, first_up, up), (sum_down, first_down, down))[direction]
        src = firsts.at[h] if n == 0 else buffers.at[h, n - 1]
        return remote(src, buffers.at[h, n], sum_sems.at[0, h, direction, n], sum_sems.at[1, h, direction, n], target)

    def weight_rows(h):
        for g in (2 * h, 2 * h + 1):
            for k in ORDER:
                row_copy(g, k, from_y(k)).wait_recv()
        return jnp.concatenate(
            [jnp.concatenate([rows[s, 2 * h], rows[s, 2 * h + 1]], axis=1) for s in range(NY)], axis=0
        )

    def weigh(h):
        row_grad = weight_rows(h)

        def partial_of(dest):
            return jnp.dot(normed[wrap(dest, NZ)], row_grad, preferred_element_type=F32)

        n_up, n_down = counts(h)
        if h == 0:
            first_up[h] = partial_of(z + n_up).astype(BF16)
            sum_copy(h, 0, 0).start()
            first_down[h] = partial_of(z - n_down).astype(BF16)
            sum_copy(h, 1, 0).start()
        else:
            first_down[h] = partial_of(z - n_down).astype(BF16)
            sum_copy(h, 1, 0).start()
            first_up[h] = partial_of(z + n_up).astype(BF16)
            sum_copy(h, 0, 0).start()
        for offset in (3, -3, 2, -2, 1, -1, 0):
            if offset not in (n_up, -n_down):
                parts[h, wrap(z + offset, NZ)] = partial_of(z + offset)

    def pass_sum(h, n):
        for direction in (h, 1 - h):
            count = counts(h)[direction]
            if n < count - 1:
                buffers = (sum_up, sum_down)[direction]
                sum_copy(h, direction, n).wait_recv()
                dest = z + (count - 1 - n) if direction == 0 else z - (count - 1 - n)
                buffers[h, n] = (buffers[h, n].astype(F32) + parts[h, wrap(dest, NZ)]).astype(BF16)
                sum_copy(h, direction, n + 1).start()

    def weights_out(h):
        n_up, n_down = counts(h)
        sum_copy(h, 0, n_up - 1).wait_recv()
        sum_copy(h, 1, n_down - 1).wait_recv()
        whole = parts[h, z] + sum_up[h, n_up - 1].astype(F32) + sum_down[h, n_down - 1].astype(F32)
        kw_ref[:, HEAD * h : HEAD * (h + 1)] = whole[:, 0:HEAD]
        vw_ref[:, HEAD * h : HEAD * (h + 1)] = whole[:, HEAD : 2 * HEAD]

    encode(0)
    launch(0)
    launch(1)
    encode(1)
    turn()
    advance(0, 0)
    advance(1, 0)
    launch(2)
    advance(0, 1)
    advance(1, 1)
    launch(3)
    advance(2, 0)
    for k in ORDER:
        turn_copy(k, from_y(k)).wait_recv()
    second_moves.step(0)
    advance(0, 2)
    advance(1, 2)
    advance(3, 0)
    advance(2, 1)
    advance(0, 3)
    advance(1, 3)
    advance(3, 1)
    second_moves.step(1)
    for copy in home[3:]:
        copy.wait()
    to_scalars.wait()
    for i in range(2):
        for k in ORDER:
            qo_copy(0, i, k, from_y(k)).wait_recv()
    score(0, 0)
    advance(2, 2)
    score(0, 1)
    advance(3, 2)
    score(0, 2)
    advance(2, 3)
    score(0, 3)
    for k in ORDER:
        stat_copy(0, k, y).start()
    advance(3, 3)
    second_moves.step(2)
    second_moves.step(3)
    for i in range(2):
        for k in ORDER:
            qo_copy(1, i, k, from_y(k)).wait_recv()
    for k in ORDER:
        stat_copy(0, k, from_y(k)).wait_recv()
    for k in (2, 1, 3, 0):
        grads_of(0, k)
    add_up(0)
    add_up(1)
    score(1, 0)
    score(1, 1)
    pass_back(0, 0)
    pass_back(1, 0)
    score(1, 2)
    score(1, 3)
    for k in ORDER:
        stat_copy(1, k, y).start()
    pass_back(0, 1)
    pass_back(1, 1)
    for k in ORDER:
        stat_copy(1, k, from_y(k)).wait_recv()
    grads_of(1, 2)
    pass_back(0, 2)
    pass_back(1, 2)
    grads_of(1, 1)
    grads_of(1, 3)
    settle(0)
    settle(1)
    grads_of(1, 0)
    add_up(2)
    add_up(3)
    second_moves.step(4)
    outputs(0)
    pass_back(2, 0)
    pass_back(3, 0)
    weigh(0)
    pass_back(2, 1)
    pass_back(3, 1)
    pass_sum(0, 0)
    pass_back(2, 2)
    pass_back(3, 2)
    pass_sum(0, 1)
    settle(2)
    settle(3)
    pass_sum(0, 2)
    outputs(1)
    weigh(1)
    weights_out(0)
    for n in range(3):
        pass_sum(1, n)
    weights_out(1)

    for k in ORDER:
        store_copy(k, y, peer(k)).wait_send()
        tab_copy(k, y).wait_send()
        turn_copy(k, y).wait_send()
        for h in range(2):
            for i in range(2):
                qo_copy(h, i, k, y).wait_send()
            stat_copy(h, k, y).wait_send()
            part_copy(h, k).wait_send()
        for g in range(4):
            row_copy(g, k, y).wait_send()
    for k in range(1, NM):
        gain_copy(k, m, wrap(m + k, NM)).wait_send()
    for direction in (0, 1):
        for g in range(4):
            for n in range(counts(g)[direction]):
                ring_sent(g, direction, n).wait_send()
                back_copy(g, direction, n).wait_send()
        for h in range(2):
            for n in range(counts(h)[direction]):
                sum_copy(h, direction, n).wait_send()


def dma(*shape):
    return pltpu.SemaphoreType.DMA(shape)


def shards(queries, out_grad, owner, store_row, store, norm_gain, w_key, w_value):
    in_smem, in_vmem, anywhere = (pl.BlockSpec(memory_space=space) for space in (SMEM, VMEM, pl.ANY))
    tile = (TOK, HEAD)
    return pl.pallas_call(
        kernel,
        out_shape=(
            jax.ShapeDtypeStruct((512, 256), BF16),
            jax.ShapeDtypeStruct((512, 256), BF16),
            jax.ShapeDtypeStruct((128, 256), F32),
            jax.ShapeDtypeStruct((128, 256), F32),
        ),
        in_specs=[in_smem, in_smem, anywhere, anywhere, anywhere, in_vmem, anywhere, anywhere],
        out_specs=(in_vmem,) * 4,
        scratch_shapes=[
            VMEM((NM, 8, TOK, 512), BF16),
            VMEM((NM, 16, 512), BF16),
            VMEM((4096, 256), BF16),
            VMEM((4096, 256), BF16),
            VMEM((NY, 8, 128), I32),
            SMEM((NY, 8, 128), I32),
            VMEM((2, NY, 2, 512, HEAD), BF16),
            VMEM((NY, 128, 256), BF16),
            VMEM((NM, 128, 1024), BF16),
        ]
        + [VMEM((64,) + tile, BF16)] * 4
        + [
            VMEM((2, NY, 4, 128, 128), F32),
            VMEM((2, NY, 4, 128, 128), F32),
            VMEM((2, NY, NY, 16, 128), F32),
            VMEM((2, 2, 512, HEAD), F32),
            VMEM((2, 3, 2, 512, HEAD), BF16),
            VMEM((2, 3, 2, 512, HEAD), BF16),
        ]
        + [VMEM((NY, REFS + 1) + tile, F32)] * 4
        + [
            VMEM((4, 64) + tile, BF16),
            VMEM((4, 4, 8) + tile, BF16),
            VMEM((4, 4, 8) + tile, BF16),
            VMEM((NY, 4, 256, HEAD), BF16),
            VMEM((2, NZ, 128, 256), F32),
            VMEM((2, 128, 256), BF16),
            VMEM((2, 128, 256), BF16),
            VMEM((2, 4, 128, 256), BF16),
            VMEM((2, 4, 128, 256), BF16),
            dma(9), dma(2, 3), dma(2, 7), dma(2, 3), dma(2, 2, 2, 3), dma(11), dma(11), dma(2, 3), dma(11), dma(11),
            dma(2, 4, 2, 4), dma(2, 2, 3), dma(2, 4, 2, 4), dma(2, 2, 3), dma(2, 4, 3), dma(2, 2, 2, 4),
        ],
        compiler_params=pltpu.CompilerParams(
            collective_id=0, has_side_effects=True, vmem_limit_bytes=60 * 1024 * 1024
        ),
        name="spans",
    )(owner.T, store_row.T, queries, out_grad, store, norm_gain, w_key, w_value)


def solution(mesh):
    in_specs = (
        P("dp", "mp"),
        P("dp", "mp"),
        P("dp", None),
        P("dp", None),
        P("dp", None, "mp"),
        P("mp"),
        P(None, "mp"),
        P(None, "mp"),
    )
    out_specs = (P("dp", "mp"), P("dp", "mp"), P("dp", "mp"), P("dp", "mp"))
    return jax.shard_map(shards, mesh=mesh, in_specs=in_specs, out_specs=out_specs, check_vma=False)
```

time: 665 us -> 131 us (0.20)
  waiting for transfers between devices: 557 us -> 0 us
  Pallas kernels: 0 us -> 123 us
  local copies, waits for them, and re-layouts: 43.8 us -> 6.47 us
  matrix products: 27.3 us -> 0 us
  between operations: 14 us -> 0.64 us
  blocking collectives: 12.3 us -> 0 us
  other arithmetic: 8.98 us -> 0 us
    reduce_scatter x2 -> x0, waiting for transfers between devices: 439 us -> none  [the longest x1 226 us: shards(): lax.psum_scatter(dense_grads.astype(jnp.bfloat16), 'dp', scatter_dimensio...]
    pallas_call x0 -> x1, Pallas kernels: none -> 123 us  [shards(): pl.pallas_call(kernel, out_shape=(jax.ShapeDtypeStruct((512, 256), BF16),...]
    all_gather x2 -> x0, waiting for transfers between devices: 117 us -> none  [the longest x1 98.6 us: shards(): everything = lax.all_gather(encoded, 'dp', axis=0, tiled=True)]
    dot_general x11 -> x0, matrix products: 27.3 us -> none  [the longest x1 5.65 us: shards(): jnp.einsum('ir,itc->rtc', placement_table, sent_grads, preferred_element_...]
    reshape x6 -> x0, local copies, waits for them, and re-layouts: 12.9 us -> none  [the longest x2 10.4 us: shards(): jnp.stack([key_grad, value_grad], axis=2)]
    all_gather x1 -> x0, blocking collectives: 12.3 us -> none  [shards(): lax.all_gather(norm_gain, 'mp', axis=0, tiled=True)]
    convert_element_type x3 -> x0, local copies, waits for them, and re-layouts: 11.9 us -> none  [the longest x1 11.3 us: shards(): dense_grads.astype(jnp.bfloat16)]
  transfers between devices with their start and end apart: 4 -> 0, of which waited for: 4 -> 0; matrix products, arithmetic and copies ran while one was open for 1% -> 0% of each run, Pallas kernels for 0% -> 0%
where the time goes in v2:
time: 131 us; the launch traced here: 130 us
  Pallas kernels  123 us (94%)
  local copies, waits for them, and re-layouts  6.47 us (5%)
    pallas_call x1, Pallas kernels, shards(): pl.pallas_call(kernel, out_shape=(jax.ShapeDtypeStruct((512, 256), BF16),...  123 us
    unnamed x4, local copies, waits for them, and re-layouts  6.47 us

profile of v2, /device:TPU:4, one launch (start us, length us, event | category | flops | bytes accessed | tf_op | source)
XLA Modules:
  0.0 129.8 jit_solution(5711822469869039645)
XLA Ops:
  0.6 122.7 %spans.1 = (bf16[512,256]{1,0:T(8,128)(2,1)}, bf16[512,256]{1,0:T(8,128)(2,1)}, f32[128,256]{1,0:T(8,128)}, f32[128,256]{1,0:T(8,128)}) custom-call(s32[2,8]{1,0:T(2,128)} %bitcast.2, s32[2,8]{1,0:T(2,128)} %bitcast.3, bf16[512,256]{1,0:T(8,128)(2,1)} %q_hbm.1, bf16[512,256]{1,0:T(8,128)(2,1)} %o_hbm.1, bf16[2,128,512]{2,1,0:T(8,128)(2,1)} %store_hbm.1, ...), custom_call_target="tpu_custom_call" | custom-call | tf_op jit(solution)/shard_map/spans/pallas_call | solution.py:585
  123.4 1.7 %copy.16 = bf16[512,256]{1,0:T(8,128)(2,1)} copy(bf16[512,256]{1,0:T(8,128)(2,1)} %get-tuple-element.8) | data formatting | bytes 524288
  125.0 1.7 %copy.17 = bf16[512,256]{1,0:T(8,128)(2,1)} copy(bf16[512,256]{1,0:T(8,128)(2,1)} %get-tuple-element.9) | data formatting | bytes 524288
  126.7 1.6 %copy.18 = f32[128,256]{1,0:T(8,128)} copy(f32[128,256]{1,0:T(8,128)} %get-tuple-element.10) | data formatting | bytes 262144
  128.3 1.6 %copy.19 = f32[128,256]{1,0:T(8,128)} copy(f32[128,256]{1,0:T(8,128)} %get-tuple-element.11) | data formatting | bytes 262144

commit v3 on v2

--- a/solution.py
+++ b/solution.py
@@ -48,16 +48,16 @@
 
 
 class MpGather:
-    def __init__(self, ref, low, high, send, recv):
-        self.ref, self.send, self.recv = ref, send, recv
+    def __init__(self, ref, base, size, send, recv, number):
+        self.ref, self.send, self.recv, self.number = ref, send, recv, number
         self.z, self.y, self.m = place()
         self.right, self.left, self.opposite = wrap(self.m + 2, NM), wrap(self.m - 2, NM), wrap(self.m + 4, NM)
         self.twin = self.m + 1 - 2 * lax.rem(self.m, 2)
-        self.low, self.high, self.whole = (0, low), (low, high - low), (0, high)
+        self.low, self.high, self.whole = (base, size // 2), (base + size // 2, size // 2), (base, size)
 
     def copy(self, block, part, target, k):
         piece = self.ref.at[block, pl.ds(*part)]
-        return remote(piece, piece, self.send.at[k], self.recv.at[k], (self.z, self.y, target))
+        return remote(piece, piece, self.send.at[self.number, k], self.recv.at[self.number, k], (self.z, self.y, target))
 
     def sent(self):
         m, left, right, opposite = self.m, self.left, self.right, self.opposite
@@ -131,8 +131,6 @@
     z, y, m = place()
     chunks, full = (g0, g1, g2, g3), (f0, f1, f2, f3)
     up, down = (wrap(z + 1, NZ), y, m), (wrap(z - 1, NZ), y, m)
-    first_moves = MpGather(every, 4, 8, every_s, every_r)
-    second_moves = MpGather(normed, 64, 128, normed_s, normed_r)
 
     def at_y(k):
         return wrap(y + k, NY)
@@ -142,6 +140,9 @@
 
     def peer(k):
         return (z, at_y(k), m)
+
+    pieces = [MpGather(every, 2 * from_y(k), 2, every_s, every_r, k) for k in range(NY)]
+    second_moves = MpGather(normed, 0, 128, normed_s, normed_r, 0)
 
     met = greet(
         [peer(k) for k in (1, 2, 3)] + [up, down] + [(z, y, wrap(m + k, NM)) for k in range(1, NM)]
@@ -208,9 +209,13 @@
     for k in ORDER:
         tab_copy(k, y).start()
     home[0].wait()
-    for k in ORDER:
+    pieces[0].step(0)
+    for k in (1, 3):
         store_copy(k, from_y(k), (z, y, m)).wait_recv()
-    first_moves.step(0)
+        pieces[k].step(0)
+    pieces[0].step(1)
+    store_copy(2, from_y(2), (z, y, m)).wait_recv()
+    pieces[2].step(0)
     for h in range(2):
         for k in ORDER:
             for i in range(2):
@@ -219,10 +224,19 @@
         tab_copy(k, from_y(k)).wait_recv()
     to_scalars = pltpu.make_async_copy(table, table_s, local.at[7])
     to_scalars.start()
-    first_moves.step(1)
-    first_moves.step(2)
-    first_moves.step(3)
-    first_moves.step(4)
+    pieces[1].step(1)
+    pieces[0].step(2)
+    pieces[3].step(1)
+    pieces[0].step(3)
+    pieces[1].step(2)
+    pieces[2].step(1)
+    pieces[3].step(2)
+    pieces[1].step(3)
+    pieces[2].step(2)
+    pieces[3].step(3)
+    pieces[2].step(3)
+    for k in (0, 1, 3, 2):
+        pieces[k].step(4)
     for k in range(1, NM):
         gain_copy(k, wrap(m - k, NM), m).wait_recv()
     home[1].wait()
@@ -407,57 +421,47 @@
         for k in ORDER:
             row_copy(g, k, y).start()
 
-    def sum_copy(h, direction, n):
+    def sum_copy(g, direction, n):
         buffers, firsts, target = ((sum_up, first_up, up), (sum_down, first_down, down))[direction]
-        src = firsts.at[h] if n == 0 else buffers.at[h, n - 1]
-        return remote(src, buffers.at[h, n], sum_sems.at[0, h, direction, n], sum_sems.at[1, h, direction, n], target)
-
-    def weight_rows(h):
-        for g in (2 * h, 2 * h + 1):
-            for k in ORDER:
-                row_copy(g, k, from_y(k)).wait_recv()
-        return jnp.concatenate(
-            [jnp.concatenate([rows[s, 2 * h], rows[s, 2 * h + 1]], axis=1) for s in range(NY)], axis=0
-        )
-
-    def weigh(h):
-        row_grad = weight_rows(h)
+        src = firsts.at[g] if n == 0 else buffers.at[g, n - 1]
+        return remote(src, buffers.at[g, n], sum_sems.at[0, g, direction, n], sum_sems.at[1, g, direction, n], target)
+
+    def weigh(g):
+        for k in ORDER:
+            row_copy(g, k, from_y(k)).wait_recv()
+        row_grad = jnp.concatenate([rows[s, g] for s in range(NY)], axis=0)
 
         def partial_of(dest):
             return jnp.dot(normed[wrap(dest, NZ)], row_grad, preferred_element_type=F32)
 
-        n_up, n_down = counts(h)
-        if h == 0:
-            first_up[h] = partial_of(z + n_up).astype(BF16)
-            sum_copy(h, 0, 0).start()
-            first_down[h] = partial_of(z - n_down).astype(BF16)
-            sum_copy(h, 1, 0).start()
-        else:
-            first_down[h] = partial_of(z - n_down).astype(BF16)
-            sum_copy(h, 1, 0).start()
-            first_up[h] = partial_of(z + n_up).astype(BF16)
-            sum_copy(h, 0, 0).start()
+        n_up, n_down = counts(g)
+        for direction in (g % 2, 1 - g % 2):
+            if direction == 0:
+                first_up[g] = partial_of(z + n_up).astype(BF16)
+            else:
+                first_down[g] = partial_of(z - n_down).astype(BF16)
+            sum_copy(g, direction, 0).start()
         for offset in (3, -3, 2, -2, 1, -1, 0):
             if offset not in (n_up, -n_down):
-                parts[h, wrap(z + offset, NZ)] = partial_of(z + offset)
-
-    def pass_sum(h, n):
-        for direction in (h, 1 - h):
-            count = counts(h)[direction]
+                parts[g, wrap(z + offset, NZ)] = partial_of(z + offset)
+
+    def pass_sum(g, n):
+        for direction in (g % 2, 1 - g % 2):
+            count = counts(g)[direction]
             if n < count - 1:
                 buffers = (sum_up, sum_down)[direction]
-                sum_copy(h, direction, n).wait_recv()
+                sum_copy(g, direction, n).wait_recv()
                 dest = z + (count - 1 - n) if direction == 0 else z - (count - 1 - n)
-                buffers[h, n] = (buffers[h, n].astype(F32) + parts[h, wrap(dest, NZ)]).astype(BF16)
-                sum_copy(h, direction, n + 1).start()
-
-    def weights_out(h):
-        n_up, n_down = counts(h)
-        sum_copy(h, 0, n_up - 1).wait_recv()
-        sum_copy(h, 1, n_down - 1).wait_recv()
-        whole = parts[h, z] + sum_up[h, n_up - 1].astype(F32) + sum_down[h, n_down - 1].astype(F32)
-        kw_ref[:, HEAD * h : HEAD * (h + 1)] = whole[:, 0:HEAD]
-        vw_ref[:, HEAD * h : HEAD * (h + 1)] = whole[:, HEAD : 2 * HEAD]
+                buffers[g, n] = (buffers[g, n].astype(F32) + parts[g, wrap(dest, NZ)]).astype(BF16)
+                sum_copy(g, direction, n + 1).start()
+
+    def weights_out(g):
+        n_up, n_down = counts(g)
+        sum_copy(g, 0, n_up - 1).wait_recv()
+        sum_copy(g, 1, n_down - 1).wait_recv()
+        whole = parts[g, z] + sum_up[g, n_up - 1].astype(F32) + sum_down[g, n_down - 1].astype(F32)
+        ref, first_column = (kw_ref, vw_ref)[g % 2], HEAD * (g // 2)
+        ref[:, first_column : first_column + HEAD] = whole
 
     encode(0)
     launch(0)
@@ -481,7 +485,6 @@
     advance(0, 3)
     advance(1, 3)
     advance(3, 1)
-    second_moves.step(1)
     for copy in home[3:]:
         copy.wait()
     to_scalars.wait()
@@ -493,64 +496,74 @@
     score(0, 1)
     advance(3, 2)
     score(0, 2)
+    score(0, 3)
+    for k in ORDER:
+        stat_copy(0, k, y).start()
     advance(2, 3)
-    score(0, 3)
-    for k in ORDER:
-        stat_copy(0, k, y).start()
     advance(3, 3)
-    second_moves.step(2)
-    second_moves.step(3)
     for i in range(2):
         for k in ORDER:
             qo_copy(1, i, k, from_y(k)).wait_recv()
+    for k in range(NY):
+        score(1, k)
+    for k in ORDER:
+        stat_copy(1, k, y).start()
     for k in ORDER:
         stat_copy(0, k, from_y(k)).wait_recv()
     for k in (2, 1, 3, 0):
         grads_of(0, k)
     add_up(0)
     add_up(1)
-    score(1, 0)
-    score(1, 1)
+    second_moves.step(1)
+    for k in ORDER:
+        stat_copy(1, k, from_y(k)).wait_recv()
+    grads_of(1, 2)
+    grads_of(1, 1)
     pass_back(0, 0)
     pass_back(1, 0)
-    score(1, 2)
-    score(1, 3)
-    for k in ORDER:
-        stat_copy(1, k, y).start()
+    grads_of(1, 3)
+    grads_of(1, 0)
     pass_back(0, 1)
     pass_back(1, 1)
-    for k in ORDER:
-        stat_copy(1, k, from_y(k)).wait_recv()
-    grads_of(1, 2)
+    add_up(2)
+    add_up(3)
+    second_moves.step(2)
+    second_moves.step(3)
     pass_back(0, 2)
     pass_back(1, 2)
-    grads_of(1, 1)
-    grads_of(1, 3)
+    pass_back(2, 0)
+    pass_back(3, 0)
     settle(0)
     settle(1)
-    grads_of(1, 0)
-    add_up(2)
-    add_up(3)
     second_moves.step(4)
-    outputs(0)
-    pass_back(2, 0)
-    pass_back(3, 0)
-    weigh(0)
     pass_back(2, 1)
     pass_back(3, 1)
-    pass_sum(0, 0)
+    weigh(0)
+    weigh(1)
     pass_back(2, 2)
     pass_back(3, 2)
-    pass_sum(0, 1)
+    pass_sum(0, 0)
+    pass_sum(1, 0)
     settle(2)
     settle(3)
+    pass_sum(0, 1)
+    pass_sum(1, 1)
+    outputs(0)
+    outputs(1)
+    weigh(2)
+    weigh(3)
     pass_sum(0, 2)
-    outputs(1)
-    weigh(1)
+    pass_sum(1, 2)
+    pass_sum(2, 0)
+    pass_sum(3, 0)
     weights_out(0)
-    for n in range(3):
-        pass_sum(1, n)
     weights_out(1)
+    pass_sum(2, 1)
+    pass_sum(3, 1)
+    pass_sum(2, 2)
+    pass_sum(3, 2)
+    weights_out(2)
+    weights_out(3)
 
     for k in ORDER:
         store_copy(k, y, peer(k)).wait_send()
@@ -570,9 +583,12 @@
             for n in range(counts(g)[direction]):
                 ring_sent(g, direction, n).wait_send()
                 back_copy(g, direction, n).wait_send()
-        for h in range(2):
-            for n in range(counts(h)[direction]):
-                sum_copy(h, direction, n).wait_send()
+                sum_copy(g, direction, n).wait_send()
+
+
+def hand_over(*refs):
+    for source, target in zip(refs[:4], refs[4:]):
+        target[...] = source[...]
 
 
 def dma(*shape):
@@ -582,7 +598,7 @@
 def shards(queries, out_grad, owner, store_row, store, norm_gain, w_key, w_value):
     in_smem, in_vmem, anywhere = (pl.BlockSpec(memory_space=space) for space in (SMEM, VMEM, pl.ANY))
     tile = (TOK, HEAD)
-    return pl.pallas_call(
+    results = pl.pallas_call(
         kernel,
         out_shape=(
             jax.ShapeDtypeStruct((512, 256), BF16),
@@ -618,19 +634,26 @@
             VMEM((4, 4, 8) + tile, BF16),
             VMEM((4, 4, 8) + tile, BF16),
             VMEM((NY, 4, 256, HEAD), BF16),
-            VMEM((2, NZ, 128, 256), F32),
-            VMEM((2, 128, 256), BF16),
-            VMEM((2, 128, 256), BF16),
-            VMEM((2, 4, 128, 256), BF16),
-            VMEM((2, 4, 128, 256), BF16),
-            dma(9), dma(2, 3), dma(2, 7), dma(2, 3), dma(2, 2, 2, 3), dma(11), dma(11), dma(2, 3), dma(11), dma(11),
-            dma(2, 4, 2, 4), dma(2, 2, 3), dma(2, 4, 2, 4), dma(2, 2, 3), dma(2, 4, 3), dma(2, 2, 2, 4),
+            VMEM((4, NZ, 128, HEAD), F32),
+            VMEM((4, 128, HEAD), BF16),
+            VMEM((4, 128, HEAD), BF16),
+            VMEM((4, 4, 128, HEAD), BF16),
+            VMEM((4, 4, 128, HEAD), BF16),
+            dma(9), dma(2, 3), dma(2, 7), dma(2, 3), dma(2, 2, 2, 3), dma(4, 11), dma(4, 11), dma(2, 3), dma(1, 11), dma(1, 11),
+            dma(2, 4, 2, 4), dma(2, 2, 3), dma(2, 4, 2, 4), dma(2, 2, 3), dma(2, 4, 3), dma(2, 4, 2, 4),
         ],
         compiler_params=pltpu.CompilerParams(
             collective_id=0, has_side_effects=True, vmem_limit_bytes=60 * 1024 * 1024
         ),
         name="spans",
     )(owner.T, store_row.T, queries, out_grad, store, norm_gain, w_key, w_value)
+    return pl.pallas_call(
+        hand_over,
+        out_shape=tuple(jax.ShapeDtypeStruct(each.shape, each.dtype) for each in results),
+        in_specs=[in_vmem] * 4,
+        out_specs=(in_vmem,) * 4,
+        name="hand_over",
+    )(*results)
 
 
 def solution(mesh):

time: 131 us -> 116 us (0.89)
  Pallas kernels: 123 us -> 115 us
  local copies, waits for them, and re-layouts: 6.47 us -> 0 us
    pallas_call x1, Pallas kernels: 123 us -> 113 us  [shards(): pl.pallas_call(kernel, out_shape=(jax.ShapeDtypeStruct((512, 256), BF16),...]
    unnamed x4 -> x0, local copies, waits for them, and re-layouts: 6.47 us -> none
    pallas_call x0 -> x1, Pallas kernels: none -> 1.99 us  [shards(): pl.pallas_call(hand_over, out_shape=tuple((jax.ShapeDtypeStruct(each.shap...]
where the time goes in v3:
time: 116 us
  Pallas kernels  115 us (99%)
    pallas_call x1, Pallas kernels, shards(): pl.pallas_call(kernel, out_shape=(jax.ShapeDtypeStruct((512, 256), BF16),...  113 us

profile of v3, /device:TPU:4, one launch (start us, length us, event | category | flops | bytes accessed | tf_op | source)
XLA Modules:
  0.0 115.7 jit_solution(6038333204666372806)
XLA Ops:
  0.6 113.1 %spans.1 = (bf16[512,256]{1,0:T(8,128)(2,1)}, bf16[512,256]{1,0:T(8,128)(2,1)}, f32[128,256]{1,0:T(8,128)}, f32[128,256]{1,0:T(8,128)}) custom-call(s32[2,8]{1,0:T(2,128)} %bitcast.2, s32[2,8]{1,0:T(2,128)} %bitcast.3, bf16[512,256]{1,0:T(8,128)(2,1)} %q_hbm.1, bf16[512,256]{1,0:T(8,128)(2,1)} %o_hbm.1, bf16[2,128,512]{2,1,0:T(8,128)(2,1)} %store_hbm.1, ...), custom_call_target="tpu_custom_call" | custom-call | tf_op jit(solution)/shard_map/spans/pallas_call | solution.py:601
  113.7 2.0 %hand_over.1 = (bf16[512,256]{1,0:T(8,128)(2,1)}, bf16[512,256]{1,0:T(8,128)(2,1)}, f32[128,256]{1,0:T(8,128)}, f32[128,256]{1,0:T(8,128)}) custom-call(bf16[512,256]{1,0:T(8,128)(2,1)} %get-tuple-element.8.refs_0_, bf16[512,256]{1,0:T(8,128)(2,1)} %get-tuple-element.9.refs_1_, f32[128,256]{1,0:T(8,128)} %get-tuple-element.10.refs_2_, ...), custom_call_target="tpu_custom_call" | custom-call | tf_op jit(solution)/shard_map/hand_over/pallas_call | solution.py:650

commit v4 on v3

v4 whole, which is shorter than its diff:
```python
import functools
import math

import jax
import jax.numpy as jnp
from jax import lax
from jax.experimental import pallas as pl
from jax.experimental.pallas import tpu as pltpu
from jax.sharding import PartitionSpec as P

MESH = pl.DeviceIdType.MESH
VMEM, SMEM = pltpu.VMEM, pltpu.SMEM
F32, BF16, I32 = jnp.float32, jnp.bfloat16, jnp.int32

HEAD = 128
ROOT = 1.0 / math.sqrt(HEAD)
EPS = 1e-06
NZ, NY, NM = 8, 4, 8
TOK = 32
REFS = 16
NONE = REFS
FLOOR = -3.0e38
DOWN = (((1,), (1,)), ((), ()))
ACROSS = (((0,), (0,)), ((), ()))
ORDER = (1, 3, 2)


def wrap(value, size):
    return lax.rem(value + size, size)


def place():
    d, m = lax.axis_index("dp"), lax.axis_index("mp")
    return lax.div(d, NY), lax.rem(d, NY), m


def remote(src, dst, send, recv, target):
    z, y, m = target
    return pltpu.make_async_remote_copy(
        src_ref=src, dst_ref=dst, send_sem=send, recv_sem=recv, device_id=(z * NY + y, m), device_id_type=MESH
    )


def greet(peers):
    barrier = pltpu.get_barrier_semaphore()
    for z, y, m in peers:
        pl.semaphore_signal(barrier, inc=1, device_id=(z * NY + y, m), device_id_type=MESH)
    return lambda: pl.semaphore_wait(barrier, len(peers))


class MpGather:
    def __init__(self, ref, base, size, send, recv, number):
        self.ref, self.send, self.recv, self.number = ref, send, recv, number
        self.z, self.y, self.m = place()
        self.right, self.left, self.opposite = wrap(self.m + 2, NM), wrap(self.m - 2, NM), wrap(self.m + 4, NM)
        self.twin = self.m + 1 - 2 * lax.rem(self.m, 2)
        self.low, self.high, self.whole = (base, size // 2), (base + size // 2, size // 2), (base, size)

    def copy(self, block, part, target, k):
        piece = self.ref.at[block, pl.ds(*part)]
        return remote(piece, piece, self.send.at[self.number, k], self.recv.at[self.number, k], (self.z, self.y, target))

    def sent(self):
        m, left, right, opposite = self.m, self.left, self.right, self.opposite
        return [
            (m, self.low, right), (m, self.high, right), (m, self.high, left), (m, self.low, left), (m, self.whole, self.twin),
            (left, self.low, right), (right, self.high, left),
            (left, self.whole, self.twin), (right, self.whole, self.twin),
            (opposite, self.low, self.twin), (opposite, self.high, self.twin),
        ]

    def came(self):
        left, right, opposite, twin = self.left, self.right, self.opposite, self.twin
        tl, tr, to = wrap(twin - 2, NM), wrap(twin + 2, NM), wrap(twin + 4, NM)
        return [
            (left, self.low), (left, self.high), (right, self.high), (right, self.low), (twin, self.whole),
            (opposite, self.low), (opposite, self.high),
            (tl, self.whole), (tr, self.whole), (to, self.low), (to, self.high),
        ]

    def start(self, k):
        block, part, target = self.sent()[k]
        self.copy(block, part, target, k).start()

    def arrive(self, k):
        block, part = self.came()[k]
        self.copy(block, part, self.twin, k).wait_recv()

    def finish_send(self, k):
        block, part, target = self.sent()[k]
        self.copy(block, part, target, k).wait_send()

    def step(self, number):
        if number == 0:
            for k in (0, 2, 1, 3, 4):
                self.start(k)
        elif number == 1:
            self.arrive(0)
            self.start(5)
            self.arrive(2)
            self.start(6)
        elif number == 2:
            self.arrive(1)
            self.start(7)
            self.arrive(3)
            self.start(8)
        elif number == 3:
            self.arrive(5)
            self.start(9)
            self.arrive(6)
            self.start(10)
        else:
            for k in (4, 7, 8, 9, 10):
                self.arrive(k)
            for k in range(11):
                self.finish_send(k)


def counts(g):
    return (4, 3) if g % 2 == 0 else (3, 4)


def kernel(
    owner_hbm, row_hbm, q_hbm, o_hbm, store_hbm, gain_ref, key_hbm, value_hbm,
    att_hbm, qg_hbm, kw_hbm, vw_hbm,
    owner_s, row_s, done_part, done_weights,
    every, gains, w_key, w_value, table, table_s, qo, turned, normed, held_k, held_v,
    e_buf, pg_buf, stats, moments, own_part, sent_part, came_part, f0, f1, f2, f3,
    dense, ring_up, ring_down, rows, parts, first_up, first_down, sum_up, sum_down,
    local, out_sems, store_sems, gain_sems, tab_sems, qo_sems, every_s, every_r, turn_sems, normed_s, normed_r,
    ring_sems, stat_sems, moment_sems, back_sems, part_sems, row_sems, sum_sems,
):
    z, y, m = place()
    full = (f0, f1, f2, f3)
    up, down = (wrap(z + 1, NZ), y, m), (wrap(z - 1, NZ), y, m)

    def at_y(k):
        return wrap(y + k, NY)

    def from_y(k):
        return wrap(y - k, NY)

    def peer(k):
        return (z, at_y(k), m)

    pieces = [MpGather(every, 2 * from_y(k), 2, every_s, every_r, k) for k in range(NY)]
    second_moves = MpGather(normed, 0, 128, normed_s, normed_r, 0)

    met = greet(
        [peer(k) for k in (1, 2, 3)] + [up, down] + [(z, y, wrap(m + k, NM)) for k in range(1, NM)]
    )

    def at_home():
        quarter = pl.ds(pl.multiple_of(TOK * y, TOK), TOK)
        copies = [
            pltpu.make_async_copy(store_hbm.at[:, quarter], every.at[m, pl.ds(2 * y, 2)], local.at[0]),
            pltpu.make_async_copy(key_hbm, w_key, local.at[1]),
            pltpu.make_async_copy(value_hbm, w_value, local.at[2]),
            pltpu.make_async_copy(owner_hbm, owner_s, local.at[9]),
            pltpu.make_async_copy(row_hbm, row_s, local.at[10]),
        ]
        for h in range(2):
            for i, ref in enumerate((q_hbm, o_hbm)):
                copies.append(
                    pltpu.make_async_copy(ref.at[:, pl.ds(HEAD * h, HEAD)], qo.at[h, y, i], local.at[3 + 2 * h + i])
                )
        return copies

    home = at_home()
    for i in (0, 3, 4, 1, 2, 5, 6, 7, 8):
        home[i].start()

    def store_copy(k, source, target):
        quarter = pl.ds(pl.multiple_of(TOK * target[1], TOK), TOK)
        return remote(
            store_hbm.at[:, quarter], every.at[m, pl.ds(2 * source, 2)], store_sems.at[0, k - 1], store_sems.at[1, k - 1], target
        )

    def gain_copy(k, source, target):
        return remote(gains.at[source], gains.at[source], gain_sems.at[0, k - 1], gain_sems.at[1, k - 1], (z, y, target))

    def tab_copy(k, source):
        return remote(table.at[source], table.at[source], tab_sems.at[0, k - 1], tab_sems.at[1, k - 1], peer(k))

    def qo_copy(h, i, k, source):
        ref = (q_hbm, o_hbm)[i]
        return remote(
            ref.at[:, pl.ds(HEAD * h, HEAD)], qo.at[h, source, i], qo_sems.at[0, h, i, k - 1], qo_sems.at[1, h, i, k - 1], peer(k)
        )

    met()
    for k in ORDER:
        store_copy(k, y, peer(k)).start()
    home[0].wait()
    pieces[0].step(0)

    home[3].wait()
    home[4].wait()

    lane = lax.broadcasted_iota(I32, (8, 128), 1)
    line = lax.broadcasted_iota(I32, (8, 128), 0)
    ids = jnp.zeros((8, 128), I32)
    first = jnp.full((8, 128), NONE, I32)
    last = jnp.full((8, 128), -1, I32)
    for r in range(REFS):
        name = owner_s[r % 2, r // 2] * 2 + row_s[r % 2, r // 2]
        ids = jnp.where(lane == r, name, ids)
        first = jnp.where(lane == name, jnp.minimum(first, r), first)
        last = jnp.where(lane == name, r, last)
    second = jnp.where(last > first, last, NONE)
    table[y] = jnp.where(line == 0, ids, jnp.where(line == 1, first, second))
    gains[m] = jnp.broadcast_to(gain_ref[...].reshape(1, 512), (16, 512))
    for g in range(4):
        full[g][:, NONE] = jnp.zeros((NY, TOK, HEAD), F32)
    moments[y] = jnp.zeros((2, NY, 8, 128), F32)

    for k in range(1, NM):
        gain_copy(k, m, wrap(m + k, NM)).start()
    for k in ORDER:
        tab_copy(k, y).start()

    def encode(k):
        first = 2 * from_y(k)
        total = jnp.zeros((64, 1), F32)
        for j in range(NM):
            part = every[j, pl.ds(first, 2)].reshape(64, 512).astype(F32)
            total += jnp.sum(part * part, axis=-1, keepdims=True)
        scale = lax.rsqrt(total * (1.0 / 4096.0) + EPS)
        keys, values = jnp.zeros((64, 256), F32), jnp.zeros((64, 256), F32)
        for j in range(NM):
            gain = gains[j][0:1].astype(F32)
            rows_of = (every[j, pl.ds(first, 2)].reshape(64, 512).astype(F32) * scale * gain).astype(BF16)
            every[j, pl.ds(first, 2)] = rows_of.reshape(2, TOK, 512)
            depth = slice(512 * j, 512 * (j + 1))
            keys += jnp.dot(rows_of, w_key[depth], preferred_element_type=F32)
            values += jnp.dot(rows_of, w_value[depth], preferred_element_type=F32)
        for h in range(2):
            for held, encoded in ((held_k, keys), (held_v, values)):
                part = encoded[:, HEAD * h : HEAD * (h + 1)].astype(BF16)
                held[h, pl.ds(8 * z + first, 2)] = part.reshape(2, TOK, HEAD)

    def ring_copy(k, i, direction, h, block):
        piece = (held_k, held_v)[i].at[:, pl.ds(8 * block + 2 * from_y(k), 2)]
        sems = [ring_sems.at[end, 4 * i + k, direction, h] for end in (0, 1)]
        return remote(piece, piece, sems[0], sems[1], (up, down)[direction])

    def ring_sent(k, i, direction, h):
        return ring_copy(k, i, direction, h, wrap(z - h, NZ) if direction == 0 else wrap(z + h, NZ))

    def ring_came(k, i, direction, h):
        return ring_copy(k, i, direction, h, wrap(z - 1 - h, NZ) if direction == 0 else wrap(z + 1 + h, NZ))

    def launch(k, i):
        for direction in (0, 1):
            ring_sent(k, i, direction, 0).start()

    def advance(k, i, h):
        for direction in (0, 1):
            if h < counts(k)[direction]:
                ring_came(k, i, direction, h).wait_recv()
                if h + 1 < counts(k)[direction]:
                    ring_sent(k, i, direction, h + 1).start()

    def turn_copy(k, source):
        lanes = pl.ds(pl.multiple_of(256 * source, 256), 256)
        return remote(
            turned.at[at_y(k)], normed.at[m, :, lanes], turn_sems.at[0, k - 1], turn_sems.at[1, k - 1], peer(k)
        )

    def turn():
        flat = every[m].reshape(256, 512).astype(F32).T.astype(BF16)
        for i in range(NY):
            turned[i] = flat[128 * i : 128 * (i + 1)]
        for k in ORDER:
            turn_copy(k, y).start()
        copy = pltpu.make_async_copy(turned.at[y], normed.at[m, :, pl.ds(pl.multiple_of(256 * y, 256), 256)], local.at[8])
        copy.start()
        copy.wait()

    context_span = lax.div(lax.broadcasted_iota(I32, (128, 128), 0), 64)
    query_span = lax.div(lax.broadcasted_iota(I32, (128, 128), 1), 64)
    same = context_span == query_span

    def context(held, h, b, p):
        return jnp.concatenate([held[h, table_s[b, 0, 4 * p + i]] for i in range(4)], axis=0)

    def score(h, k):
        b = at_y(k)
        for p in range(4):
            queries = qo[h, b, 0, 128 * p : 128 * (p + 1)]
            scores = lax.dot_general(context(held_k, h, b, p), queries, DOWN, preferred_element_type=F32) * ROOT
            scores = jnp.where(same, scores, FLOOR)
            top = jnp.max(scores, axis=0, keepdims=True)
            weights = jnp.exp(scores - top)
            e_buf[h, k, p] = weights
            stats[y, h, b, p : p + 1] = top
            stats[y, h, b, 4 + p : 5 + p] = jnp.sum(weights, axis=0, keepdims=True)

    def stat_copy(k, source):
        piece = stats.at[source]
        return remote(piece, piece, stat_sems.at[0, k - 1], stat_sems.at[1, k - 1], peer(k))

    def moment_copy(k, source):
        piece = moments.at[source]
        return remote(piece, piece, moment_sems.at[0, k - 1], moment_sems.at[1, k - 1], peer(k))

    def part_copy(h, i, k):
        return remote(
            sent_part.at[h, i, k - 1], came_part.at[h, i, k - 1], part_sems.at[0, h, i, k - 1], part_sems.at[1, h, i, k - 1], peer(k)
        )

    def keep(h, i, k, lines, value):
        if k == 0:
            own_part[h, i, lines] = value
        else:
            sent_part[h, i, k - 1, lines] = value.astype(BF16)

    def attend(h, k):
        b = at_y(k)
        tops = [stats[s, h, b, 0:4] for s in range(NY)]
        top = jnp.maximum(jnp.maximum(tops[0], tops[1]), jnp.maximum(tops[2], tops[3]))
        whole = jnp.zeros((4, 128), F32)
        for s in range(NY):
            whole += jnp.exp(tops[s] - top) * stats[s, h, b, 4:8]
        factor = jnp.exp(stats[y, h, b, 0:4] - top) / whole
        for p in range(4):
            lines = slice(128 * p, 128 * (p + 1))
            grads = qo[h, b, 1, lines]
            values = context(held_v, h, b, p)
            probs = e_buf[h, k, p] * factor[p : p + 1]
            low = probs.astype(BF16)
            prob_grad = lax.dot_general(values, grads, DOWN, preferred_element_type=F32)
            e_buf[h, k, p] = probs
            pg_buf[h, k, p] = prob_grad
            moments[y, h, b, p : p + 1] = jnp.sum(probs * prob_grad, axis=0, keepdims=True)
            keep(h, 0, k, lines, lax.dot_general(low, values, ACROSS, preferred_element_type=F32))
            value_grad = jnp.dot(low, grads, preferred_element_type=F32)
            full[h][b, 4 * p : 4 * p + 4] = value_grad.reshape(4, TOK, HEAD)

    def grads_of(h, k):
        b = at_y(k)
        delta = (moments[0, h, b, 0:4] + moments[1, h, b, 0:4]) + (moments[2, h, b, 0:4] + moments[3, h, b, 0:4])
        for p in range(4):
            lines = slice(128 * p, 128 * (p + 1))
            score_grad = (e_buf[h, k, p] * (pg_buf[h, k, p] - delta[p : p + 1])).astype(BF16)
            keys = context(held_k, h, b, p)
            keep(h, 1, k, lines, lax.dot_general(score_grad, keys, ACROSS, preferred_element_type=F32) * ROOT)
            key_grad = jnp.dot(score_grad, qo[h, b, 0, lines], preferred_element_type=F32) * ROOT
            full[2 + h][b, 4 * p : 4 * p + 4] = key_grad.reshape(4, TOK, HEAD)

    def send_parts(h, i):
        for k in ORDER:
            part_copy(h, i, k).start()

    def outputs(h, i):
        for k in ORDER:
            part_copy(h, i, k).wait_recv()
        whole = own_part[h, i]
        for k in ORDER:
            whole += came_part[h, i, k - 1].astype(F32)
        done_part[h, i] = whole.astype(BF16)
        part_out(h, i).start()

    def part_out(h, i):
        ref = (att_hbm, qg_hbm)[i]
        return pltpu.make_async_copy(done_part.at[h, i], ref.at[:, pl.ds(HEAD * h, HEAD)], out_sems.at[2 * h + i])

    def block(dest):
        return pl.ds(8 * wrap(dest, NZ), 8)

    def back_copy(g, direction, h):
        buffers, target = ((ring_up, up), (ring_down, down))[direction]
        count = counts(g)[direction]
        if h == 0:
            src = dense.at[g, block(z + count if direction == 0 else z - count)]
        else:
            src = buffers.at[g, h - 1]
        return remote(src, buffers.at[g, h], back_sems.at[0, g, direction, h], back_sems.at[1, g, direction, h], target)

    def add_up(g):
        def body(s, carry):
            whole = full[g][0, table_s[0, 1, s]] + full[g][0, table_s[0, 2, s]]
            for b in range(1, NY):
                whole += full[g][b, table_s[b, 1, s]] + full[g][b, table_s[b, 2, s]]
            dense[g, s] = whole.astype(BF16)
            return carry

        lax.fori_loop(0, 64, body, 0, unroll=4)
        for direction in (0, 1):
            back_copy(g, direction, 0).start()

    def pass_back(g, h):
        for direction in (0, 1):
            count = counts(g)[direction]
            if h < count - 1:
                buffers = (ring_up, ring_down)[direction]
                back_copy(g, direction, h).wait_recv()
                dest = z + (count - 1 - h) if direction == 0 else z - (count - 1 - h)
                buffers[g, h] = (buffers[g, h].astype(F32) + dense[g, block(dest)].astype(F32)).astype(BF16)
                back_copy(g, direction, h + 1).start()

    def row_copy(g, k, source):
        piece = rows.at[source, g]
        return remote(piece, piece, row_sems.at[0, g, k - 1], row_sems.at[1, g, k - 1], peer(k))

    def settle(g):
        n_up, n_down = counts(g)
        back_copy(g, 0, n_up - 1).wait_recv()
        back_copy(g, 1, n_down - 1).wait_recv()
        whole = dense[g, block(z)].astype(F32) + ring_up[g, n_up - 1].astype(F32) + ring_down[g, n_down - 1].astype(F32)
        rows[y, g] = whole.astype(BF16).reshape(256, HEAD)
        for k in ORDER:
            row_copy(g, k, y).start()

    def sum_copy(g, direction, n):
        buffers, firsts, target = ((sum_up, first_up, up), (sum_down, first_down, down))[direction]
        src = firsts.at[g] if n == 0 else buffers.at[g, n - 1]
        return remote(src, buffers.at[g, n], sum_sems.at[0, g, direction, n], sum_sems.at[1, g, direction, n], target)

    def weigh(g):
        for k in ORDER:
            row_copy(g, k, from_y(k)).wait_recv()
        row_grad = jnp.concatenate([rows[s, g] for s in range(NY)], axis=0)

        def partial_of(dest):
            return jnp.dot(normed[wrap(dest, NZ)], row_grad, preferred_element_type=F32)

        n_up, n_down = counts(g)
        for direction in (g % 2, 1 - g % 2):
            if direction == 0:
                first_up[g] = partial_of(z + n_up).astype(BF16)
            else:
                first_down[g] = partial_of(z - n_down).astype(BF16)
            sum_copy(g, direction, 0).start()
        for offset in (3, -3, 2, -2, 1, -1, 0):
            if offset not in (n_up, -n_down):
                parts[g, wrap(z + offset, NZ)] = partial_of(z + offset)

    def pass_sum(g, n):
        for direction in (g % 2, 1 - g % 2):
            count = counts(g)[direction]
            if n < count - 1:
                buffers = (sum_up, sum_down)[direction]
                sum_copy(g, direction, n).wait_recv()
                dest = z + (count - 1 - n) if direction == 0 else z - (count - 1 - n)
                buffers[g, n] = (buffers[g, n].astype(F32) + parts[g, wrap(dest, NZ)]).astype(BF16)
                sum_copy(g, direction, n + 1).start()

    def weights_out(g):
        n_up, n_down = counts(g)
        sum_copy(g, 0, n_up - 1).wait_recv()
        sum_copy(g, 1, n_down - 1).wait_recv()
        whole = parts[g, z] + sum_up[g, n_up - 1].astype(F32) + sum_down[g, n_down - 1].astype(F32)
        done_weights[g] = whole
        weight_out(g).start()

    def weight_out(g):
        ref = (vw_hbm, kw_hbm)[g // 2]
        return pltpu.make_async_copy(done_weights.at[g], ref.at[:, pl.ds(HEAD * (g % 2), HEAD)], out_sems.at[4 + g])

    def arrive(k):
        store_copy(k, from_y(k), (z, y, m)).wait_recv()
        pieces[k].step(0)

    def send_queries():
        for h in range(2):
            for k in ORDER:
                for i in range(2):
                    qo_copy(h, i, k, y).start()

    def weights_here():
        for k in range(1, NM):
            gain_copy(k, wrap(m - k, NM), m).wait_recv()
        home[1].wait()
        home[2].wait()

    def finish_piece(k):
        pieces[k].step(4)
        encode(k)
        launch(k, 0)
        launch(k, 1)

    go = functools.partial
    plan = [(4.3, go(arrive, 1)), (4.5, go(arrive, 3)), (6.3, go(arrive, 2)), (6.4, send_queries), (7.0, weights_here), (17.2, turn)]
    for k, steps in ((0, (3.7, 4.4, 6.8, 8.2)), (1, (8.0, 8.7, 11.0, 12.5)), (3, (8.6, 9.3, 11.7, 13.3)), (2, (10.5, 11.2, 13.5, 15.0))):
        for number in range(3):
            plan.append((steps[number], go(pieces[k].step, number + 1)))
        plan.append((steps[3], go(finish_piece, k)))
        for h in range(4):
            due = steps[3] + 2.0 + 3.4 * (h + 1)
            plan.append((due, go(advance, k, 0, h)))
            plan.append((due + 2.0, go(advance, k, 1, h)))

    def scalars_here():
        for k in ORDER:
            tab_copy(k, from_y(k)).wait_recv()
        to_scalars = pltpu.make_async_copy(table, table_s, local.at[7])
        to_scalars.start()
        for copy in home[5:]:
            copy.wait()
        to_scalars.wait()

    def queries_here(h):
        for i in range(2):
            for k in ORDER:
                qo_copy(h, i, k, from_y(k)).wait_recv()

    def send_stats():
        for k in ORDER:
            stat_copy(k, y).start()

    def stats_here():
        for k in ORDER:
            stat_copy(k, from_y(k)).wait_recv()

    def send_moments():
        for k in ORDER:
            moment_copy(k, y).start()

    def moments_here():
        for k in ORDER:
            moment_copy(k, from_y(k)).wait_recv()

    def turned_here():
        for k in ORDER:
            turn_copy(k, from_y(k)).wait_recv()

    due = 15.0 + 2.0 + 3.4 * 4 + 0.1
    plan += [(due, scalars_here), (due, go(queries_here, 0)), (due, go(queries_here, 1))]
    plan += [(due, go(score, h, k)) for h in range(2) for k in range(NY)] + [(due, send_stats)]
    steps = [action for _, action in sorted(plan, key=lambda entry: entry[0])]
    steps += [stats_here] + [go(attend, 0, k) for k in range(NY)] + [go(add_up, 0)]
    steps += [go(attend, 1, k) for k in range(NY)] + [send_moments, go(add_up, 1), go(send_parts, 0, 0), go(send_parts, 1, 0)]
    steps += [turned_here, go(second_moves.step, 0), go(pass_back, 0, 0), go(pass_back, 1, 0), moments_here]
    for h in range(2):
        steps += [go(grads_of, h, k) for k in range(NY)] + [go(add_up, 2 + h)]
    steps += [go(send_parts, 0, 1), go(pass_back, 0, 1), go(pass_back, 1, 1), go(second_moves.step, 1)]
    steps += [go(pass_back, 2, 0), go(pass_back, 3, 0), go(pass_back, 0, 2), go(pass_back, 1, 2), go(second_moves.step, 2)]
    steps += [go(pass_back, 2, 1), go(pass_back, 3, 1), go(settle, 0), go(settle, 1), go(second_moves.step, 3)]
    steps += [go(pass_back, 2, 2), go(pass_back, 3, 2), go(second_moves.step, 4), go(outputs, 0, 0), go(settle, 2), go(settle, 3)]
    steps += [go(send_parts, 1, 1), go(outputs, 1, 0), go(weigh, 0), go(weigh, 1), go(pass_sum, 0, 0), go(pass_sum, 1, 0)]
    steps += [go(weigh, 2), go(pass_sum, 0, 1), go(pass_sum, 1, 1), go(weigh, 3), go(pass_sum, 0, 2), go(pass_sum, 1, 2)]
    steps += [go(pass_sum, 2, 0), go(pass_sum, 3, 0), go(weights_out, 0), go(weights_out, 1), go(pass_sum, 2, 1), go(pass_sum, 3, 1)]
    steps += [go(outputs, 0, 1), go(pass_sum, 2, 2), go(pass_sum, 3, 2), go(weights_out, 2), go(weights_out, 3), go(outputs, 1, 1)]
    for action in steps:
        action()

    for h in range(2):
        for i in range(2):
            part_out(h, i).wait()
    for g in range(4):
        weight_out(g).wait()
    for k in ORDER:
        store_copy(k, y, peer(k)).wait_send()
        tab_copy(k, y).wait_send()
        turn_copy(k, y).wait_send()
        stat_copy(k, y).wait_send()
        moment_copy(k, y).wait_send()
        for h in range(2):
            for i in range(2):
                qo_copy(h, i, k, y).wait_send()
                part_copy(h, i, k).wait_send()
        for g in range(4):
            row_copy(g, k, y).wait_send()
    for k in range(1, NM):
        gain_copy(k, m, wrap(m + k, NM)).wait_send()
    for direction in (0, 1):
        for g in range(4):
            for n in range(counts(g)[direction]):
                ring_sent(g, 0, direction, n).wait_send()
                ring_sent(g, 1, direction, n).wait_send()
                back_copy(g, direction, n).wait_send()
                sum_copy(g, direction, n).wait_send()


def hand_over(*refs):
    for source, target in zip(refs[:4], refs[4:]):
        target[...] = source[...]


def dma(*shape):
    return pltpu.SemaphoreType.DMA(shape)


def shards(queries, out_grad, owner, store_row, store, norm_gain, w_key, w_value):
    in_vmem, anywhere = (pl.BlockSpec(memory_space=space) for space in (VMEM, pl.ANY))
    tile = (TOK, HEAD)
    results = pl.pallas_call(
        kernel,
        out_shape=(
            jax.ShapeDtypeStruct((512, 256), BF16),
            jax.ShapeDtypeStruct((512, 256), BF16),
            jax.ShapeDtypeStruct((128, 256), F32),
            jax.ShapeDtypeStruct((128, 256), F32),
        ),
        in_specs=[anywhere, anywhere, anywhere, anywhere, anywhere, in_vmem, anywhere, anywhere],
        out_specs=(anywhere,) * 4,
        scratch_shapes=[
            SMEM((2, 8), I32),
            SMEM((2, 8), I32),
            VMEM((2, 2, 512, HEAD), BF16),
            VMEM((4, 128, HEAD), F32),
            VMEM((NM, 8, TOK, 512), BF16),
            VMEM((NM, 16, 512), BF16),
            VMEM((4096, 256), BF16),
            VMEM((4096, 256), BF16),
            VMEM((NY, 8, 128), I32),
            SMEM((NY, 8, 128), I32),
            VMEM((2, NY, 2, 512, HEAD), BF16),
            VMEM((NY, 128, 256), BF16),
            VMEM((NM, 128, 1024), BF16),
            VMEM((2, 64) + tile, BF16),
            VMEM((2, 64) + tile, BF16),
            VMEM((2, NY, 4, 128, 128), F32),
            VMEM((2, NY, 4, 128, 128), F32),
            VMEM((NY, 2, NY, 8, 128), F32),
            VMEM((NY, 2, NY, 8, 128), F32),
            VMEM((2, 2, 512, HEAD), F32),
            VMEM((2, 2, 3, 512, HEAD), BF16),
            VMEM((2, 2, 3, 512, HEAD), BF16),
        ]
        + [VMEM((NY, REFS + 1) + tile, F32)] * 4
        + [
            VMEM((4, 64) + tile, BF16),
            VMEM((4, 4, 8) + tile, BF16),
            VMEM((4, 4, 8) + tile, BF16),
            VMEM((NY, 4, 256, HEAD), BF16),
            VMEM((4, NZ, 128, HEAD), F32),
            VMEM((4, 128, HEAD), BF16),
            VMEM((4, 128, HEAD), BF16),
            VMEM((4, 4, 128, HEAD), BF16),
            VMEM((4, 4, 128, HEAD), BF16),
            dma(11), dma(8), dma(2, 3), dma(2, 7), dma(2, 3), dma(2, 2, 2, 3), dma(4, 11), dma(4, 11), dma(2, 3), dma(1, 11), dma(1, 11),
            dma(2, 8, 2, 4), dma(2, 3), dma(2, 3), dma(2, 4, 2, 4), dma(2, 2, 2, 3), dma(2, 4, 3), dma(2, 4, 2, 4),
        ],
        compiler_params=pltpu.CompilerParams(
            collective_id=0, has_side_effects=True, vmem_limit_bytes=60 * 1024 * 1024
        ),
        name="spans",
    )(owner.T, store_row.T, queries, out_grad, store, norm_gain, w_key, w_value)
    return pl.pallas_call(
        hand_over,
        out_shape=tuple(jax.ShapeDtypeStruct(each.shape, each.dtype) for each in results),
        in_specs=[in_vmem] * 4,
        out_specs=(in_vmem,) * 4,
        name="hand_over",
    )(*results)


def solution(mesh):
    in_specs = (
        P("dp", "mp"),
        P("dp", "mp"),
        P("dp", None),
        P("dp", None),
        P("dp", None, "mp"),
        P("mp"),
        P(None, "mp"),
        P(None, "mp"),
    )
    out_specs = (P("dp", "mp"), P("dp", "mp"), P("dp", "mp"), P("dp", "mp"))
    return jax.shard_map(shards, mesh=mesh, in_specs=in_specs, out_specs=out_specs, check_vma=False)
```

time: 116 us -> 107 us (0.922)
  Pallas kernels: 115 us -> 106 us
    pallas_call x1, Pallas kernels: 113 us -> 104 us  [shards(): pl.pallas_call(kernel, out_shape=(jax.ShapeDtypeStruct((512, 256), BF16),...]
where the time goes in v4:
time: 107 us; the launch traced here: 106 us
  Pallas kernels  106 us (99%)
    pallas_call x1, Pallas kernels, shards(): pl.pallas_call(kernel, out_shape=(jax.ShapeDtypeStruct((512, 256), BF16),...  104 us

profile of v4, /device:TPU:4, one launch (start us, length us, event | category | flops | bytes accessed | tf_op | source)
XLA Modules:
  0.0 106.4 jit_solution(8610045788404442283)
XLA Ops:
  0.6 103.7 %spans.1 = (bf16[512,256]{1,0:T(8,128)(2,1)}, bf16[512,256]{1,0:T(8,128)(2,1)}, f32[128,256]{1,0:T(8,128)}, f32[128,256]{1,0:T(8,128)}) custom-call(s32[2,8]{1,0:T(2,128)} %bitcast.2, s32[2,8]{1,0:T(2,128)} %bitcast.3, bf16[512,256]{1,0:T(8,128)(2,1)} %q_hbm.1, bf16[512,256]{1,0:T(8,128)(2,1)} %o_hbm.1, bf16[2,128,512]{2,1,0:T(8,128)(2,1)} %store_hbm.1, ...), custom_call_target="tpu_custom_call" | custom-call | tf_op jit(solution)/shard_map/spans/pallas_call | solution.py:588
  104.4 2.0 %hand_over.1 = (bf16[512,256]{1,0:T(8,128)(2,1)}, bf16[512,256]{1,0:T(8,128)(2,1)}, f32[128,256]{1,0:T(8,128)}, f32[128,256]{1,0:T(8,128)}) custom-call(bf16[512,256]{1,0:T(8,128)(2,1)} %get-tuple-element.8.refs_0_, bf16[512,256]{1,0:T(8,128)(2,1)} %get-tuple-element.9.refs_1_, f32[128,256]{1,0:T(8,128)} %get-tuple-element.10.refs_2_, ...), custom_call_target="tpu_custom_call" | custom-call | tf_op jit(solution)/shard_map/hand_over/pallas_call | solution.py:641

commit v5 on v4

--- a/solution.py
+++ b/solution.py
@@ -112,8 +112,10 @@
         else:
             for k in (4, 7, 8, 9, 10):
                 self.arrive(k)
-            for k in range(11):
-                self.finish_send(k)
+
+    def finish(self):
+        for k in range(11):
+            self.finish_send(k)
 
 
 def counts(g):
@@ -124,7 +126,7 @@
     owner_hbm, row_hbm, q_hbm, o_hbm, store_hbm, gain_ref, key_hbm, value_hbm,
     att_hbm, qg_hbm, kw_hbm, vw_hbm,
     owner_s, row_s, done_part, done_weights,
-    every, gains, w_key, w_value, table, table_s, qo, turned, normed, held_k, held_v,
+    every, kept, gains, w_key, w_value, table, table_s, qo, turned, normed, held_k, held_v,
     e_buf, pg_buf, stats, moments, own_part, sent_part, came_part, f0, f1, f2, f3,
     dense, ring_up, ring_down, rows, parts, first_up, first_down, sum_up, sum_down,
     local, out_sems, store_sems, gain_sems, tab_sems, qo_sems, every_s, every_r, turn_sems, normed_s, normed_r,
@@ -230,7 +232,7 @@
         for j in range(NM):
             gain = gains[j][0:1].astype(F32)
             rows_of = (every[j, pl.ds(first, 2)].reshape(64, 512).astype(F32) * scale * gain).astype(BF16)
-            every[j, pl.ds(first, 2)] = rows_of.reshape(2, TOK, 512)
+            kept[j, pl.ds(first, 2)] = rows_of.reshape(2, TOK, 512)
             depth = slice(512 * j, 512 * (j + 1))
             keys += jnp.dot(rows_of, w_key[depth], preferred_element_type=F32)
             values += jnp.dot(rows_of, w_value[depth], preferred_element_type=F32)
@@ -268,7 +270,7 @@
         )
 
     def turn():
-        flat = every[m].reshape(256, 512).astype(F32).T.astype(BF16)
+        flat = kept[m].reshape(256, 512).astype(F32).T.astype(BF16)
         for i in range(NY):
             turned[i] = flat[128 * i : 128 * (i + 1)]
         for k in ORDER:
@@ -534,17 +536,19 @@
     steps += [turned_here, go(second_moves.step, 0), go(pass_back, 0, 0), go(pass_back, 1, 0), moments_here]
     for h in range(2):
         steps += [go(grads_of, h, k) for k in range(NY)] + [go(add_up, 2 + h)]
-    steps += [go(send_parts, 0, 1), go(pass_back, 0, 1), go(pass_back, 1, 1), go(second_moves.step, 1)]
-    steps += [go(pass_back, 2, 0), go(pass_back, 3, 0), go(pass_back, 0, 2), go(pass_back, 1, 2), go(second_moves.step, 2)]
+    steps += [go(send_parts, 0, 1), go(pass_back, 0, 1), go(pass_back, 1, 1)]
+    steps += [go(pass_back, 2, 0), go(pass_back, 3, 0), go(pass_back, 0, 2), go(pass_back, 1, 2), go(second_moves.step, 1), go(second_moves.step, 2)]
     steps += [go(pass_back, 2, 1), go(pass_back, 3, 1), go(settle, 0), go(settle, 1), go(second_moves.step, 3)]
-    steps += [go(pass_back, 2, 2), go(pass_back, 3, 2), go(second_moves.step, 4), go(outputs, 0, 0), go(settle, 2), go(settle, 3)]
-    steps += [go(send_parts, 1, 1), go(outputs, 1, 0), go(weigh, 0), go(weigh, 1), go(pass_sum, 0, 0), go(pass_sum, 1, 0)]
-    steps += [go(weigh, 2), go(pass_sum, 0, 1), go(pass_sum, 1, 1), go(weigh, 3), go(pass_sum, 0, 2), go(pass_sum, 1, 2)]
+    steps += [go(pass_back, 2, 2), go(pass_back, 3, 2), go(second_moves.step, 4), go(settle, 2), go(weigh, 0), go(settle, 3)]
+    steps += [go(weigh, 1), go(pass_sum, 0, 0), go(outputs, 0, 0), go(outputs, 1, 0), go(pass_sum, 1, 0)]
+    steps += [go(weigh, 2), go(pass_sum, 0, 1), go(pass_sum, 1, 1), go(weigh, 3), go(send_parts, 1, 1), go(pass_sum, 0, 2), go(pass_sum, 1, 2)]
     steps += [go(pass_sum, 2, 0), go(pass_sum, 3, 0), go(weights_out, 0), go(weights_out, 1), go(pass_sum, 2, 1), go(pass_sum, 3, 1)]
     steps += [go(outputs, 0, 1), go(pass_sum, 2, 2), go(pass_sum, 3, 2), go(weights_out, 2), go(weights_out, 3), go(outputs, 1, 1)]
     for action in steps:
         action()
 
+    for moves in pieces + [second_moves]:
+        moves.finish()
     for h in range(2):
         for i in range(2):
             part_out(h, i).wait()
@@ -600,6 +604,7 @@
             SMEM((2, 8), I32),
             VMEM((2, 2, 512, HEAD), BF16),
             VMEM((4, 128, HEAD), F32),
+            VMEM((NM, 8, TOK, 512), BF16),
             VMEM((NM, 8, TOK, 512), BF16),
             VMEM((NM, 16, 512), BF16),
             VMEM((4096, 256), BF16),

time: 107 us -> 106 us (level)
  no operation moved by 1% of the time
where the time goes in v5:
time: 106 us
  Pallas kernels  105 us (99%)
    pallas_call x1, Pallas kernels, shards(): pl.pallas_call(kernel, out_shape=(jax.ShapeDtypeStruct((512, 256), BF16),...  103 us

profile of v5, /device:TPU:4, one launch (start us, length us, event | category | flops | bytes accessed | tf_op | source)
XLA Modules:
  0.0 105.8 jit_solution(12607514374351382901)
XLA Ops:
  0.6 103.2 %spans.1 = (bf16[512,256]{1,0:T(8,128)(2,1)}, bf16[512,256]{1,0:T(8,128)(2,1)}, f32[128,256]{1,0:T(8,128)}, f32[128,256]{1,0:T(8,128)}) custom-call(s32[2,8]{1,0:T(2,128)} %bitcast.2, s32[2,8]{1,0:T(2,128)} %bitcast.3, bf16[512,256]{1,0:T(8,128)(2,1)} %q_hbm.1, bf16[512,256]{1,0:T(8,128)(2,1)} %o_hbm.1, bf16[2,128,512]{2,1,0:T(8,128)(2,1)} %store_hbm.1, ...), custom_call_target="tpu_custom_call" | custom-call | tf_op jit(solution)/shard_map/spans/pallas_call | solution.py:592
  103.8 2.0 %hand_over.1 = (bf16[512,256]{1,0:T(8,128)(2,1)}, bf16[512,256]{1,0:T(8,128)(2,1)}, f32[128,256]{1,0:T(8,128)}, f32[128,256]{1,0:T(8,128)}) custom-call(bf16[512,256]{1,0:T(8,128)(2,1)} %get-tuple-element.8.refs_0_, bf16[512,256]{1,0:T(8,128)(2,1)} %get-tuple-element.9.refs_1_, f32[128,256]{1,0:T(8,128)} %get-tuple-element.10.refs_2_, ...), custom_call_target="tpu_custom_call" | custom-call | tf_op jit(solution)/shard_map/hand_over/pallas_call | solution.py:646
